TPU v7x, 32 devices: a whole 2x2x4 slice. The times are simulated.
32 devices in a mesh: seq: 8 (over y, x, core), tp: 4 (over z).
Axes of the slice: x: 2, y: 2, z: 4, core: 2. Of those that a mesh axis runs over, the one named last changes fastest.
Arguments:
- block_input: bfloat16 [4096, 1024], P('seq'), may hold values from -6 to 6
- scene_lengths: int32 [4], replicated, may hold values from 1 to 4096, as said below
- input_gain: float32 [1024], replicated, may hold values from 0.5 to 1.5
- gate_weight: bfloat16 [1024, 2048], P(None, 'tp'), may hold values from -0.1875 to 0.1875
- inner_weight: bfloat16 [1024, 2048], P(None, 'tp'), may hold values from -0.1875 to 0.1875
- state_weight: bfloat16 [1024, 256], P(None, 'tp'), may hold values from -0.1875 to 0.1875
- step_weight: bfloat16 [1024, 32], P(None, 'tp'), may hold values from -0.1875 to 0.1875
- step_bias: float32 [32], P('tp'), may hold values from -1.5 to 1
- rate_log: float32 [32], P('tp'), may hold values from -9 to -3.5
- inner_kernel: float32 [4, 2048], P(None, 'tp'), may hold values from -3 to 3
- inner_conv_bias: float32 [2048], P('tp'), may hold values from -2 to 2
- state_kernel: float32 [4, 256], P(None, 'tp'), may hold values from -3 to 3
- state_conv_bias: float32 [256], P('tp'), may hold values from -2 to 2
- skip_scale: float32 [32], P('tp'), may hold values from 1 to 8
- gate_gain: float32 [2048], P('tp'), may hold values from 0.5 to 1.5
- out_weight: bfloat16 [2048, 1024], P('tp'), may hold values from -0.125 to 0.125
- out_cotangent: bfloat16 [4096, 1024], P('seq'), may hold values from -6 to 6
Outputs:
- block_output: bfloat16 [4096, 1024], P('seq')
- input_grad: float32 [4096, 1024], P('seq')
- input_gain_grad: float32 [1024], replicated
- gate_weight_grad: float32 [1024, 2048], P('seq', 'tp')
- inner_weight_grad: float32 [1024, 2048], P('seq', 'tp')
- state_weight_grad: float32 [1024, 256], P('seq', 'tp')
- step_weight_grad: float32 [1024, 32], P('seq', 'tp')
- step_bias_grad: float32 [32], P('tp')
- rate_log_grad: float32 [32], P('tp')
- inner_kernel_grad: float32 [4, 2048], P(None, 'tp')
- inner_conv_bias_grad: float32 [2048], P('tp')
- state_kernel_grad: float32 [4, 256], P(None, 'tp')
- state_conv_bias_grad: float32 [256], P('tp')
- skip_scale_grad: float32 [32], P('tp')
- gate_gain_grad: float32 [2048], P('tp')
- out_weight_grad: float32 [2048, 1024], P('tp', 'seq')
Inputs may be any that keep to these rules, and one draw needn't show every extreme that they name: `scene_lengths`: the lengths sum to 4096; one scene, which one drawn from the seed, holds all but at most 384 tokens, and every other scene holds 1 to 128.
All inputs are finite; a program needn't handle non-finite values.
Results may differ from a plain program's by a relative error of at most 0.0085.
The roundings to bfloat16 on the way count: a program that leaves them out, or rounds other values in their place, can miss the bound.
Values may be sent and summed in bfloat16 or wider, within the bound.
A program may use at most 128 MiB of HBM per device.

v0:
```python
import contextlib
import functools
import types

import jax
import jax.numpy as jnp
from jax import lax
from jax.experimental import pallas as pl
from jax.experimental.pallas import tpu as pltpu
from jax.sharding import PartitionSpec as P

STATE = 128
CONV = 4
CHUNK = 256
LANES = 128
PAD = 8
ROWS = 64
epsilon = 1e-05
bf = jnp.bfloat16
f32 = jnp.float32
i32 = jnp.int32
MESH = pl.DeviceIdType.MESH


def dg(left, right, left_dim, right_dim):
    return lax.dot_general(
        left, right, (((left_dim,), (right_dim,)), ((), ())), preferred_element_type=f32
    )


def split3(v):
    high = v.astype(bf).astype(f32)
    middle = (v - high).astype(bf).astype(f32)
    return jnp.concatenate([high, middle, v - high - middle], axis=0).astype(bf)


def fold3(v):
    third = v.shape[0] // 3
    return v[:third] + v[third : 2 * third] + v[2 * third :]


def halves(v):
    high = v.astype(bf)
    return high, (v - high.astype(f32)).astype(bf)


def slope(v):
    s = jax.nn.sigmoid(v)
    return s * (1.0 + v * (1.0 - s))


def fold8(v):
    total = v[0:8]
    for i in range(1, v.shape[0] // 8):
        total = total + v[8 * i : 8 * i + 8]
    return total


def iota(shape, dim):
    return lax.broadcasted_iota(i32, shape, dim)


def kernel(sizes, names, *refs):
    r = types.SimpleNamespace(**dict(zip(names, refs)))
    n_seq, n_tp, T, D, HI, H, NS = sizes
    N = STATE
    P_ = HI // H
    Q = CHUNK
    NC = T // Q
    NP = HI // LANES
    R = HI // n_seq
    R2 = D // n_seq
    total_tokens = T * n_seq
    seq = lax.axis_index("seq")
    tp = lax.axis_index("tp")

    barrier = pltpu.get_barrier_semaphore()
    for d in range(1, n_seq):
        pl.semaphore_signal(
            barrier, inc=1, device_id=((seq + d) % n_seq, tp), device_id_type=MESH
        )
    for d in range(1, n_tp):
        pl.semaphore_signal(
            barrier, inc=1, device_id=(seq, (tp + d) % n_tp), device_id_type=MESH
        )

    waits = []
    marks = contextlib.ExitStack()

    def stage(name):
        marks.close()
        marks.enter_context(jax.named_scope(name))

    stage("norm")

    def remote(src, dst, send, recv, device):
        return pltpu.make_async_remote_copy(
            src_ref=src,
            dst_ref=dst,
            send_sem=send,
            recv_sem=recv,
            device_id=device,
            device_id_type=MESH,
        )

    def spread(axis, src_to, dst_from, send, recv):
        n = n_seq if axis == "seq" else n_tp
        me = seq if axis == "seq" else tp
        incoming = []
        for d in range(1, n):
            target = (me + d) % n
            source = (me + n - d) % n
            device = (target, tp) if axis == "seq" else (seq, target)
            out = remote(src_to(target), dst_from(me), send.at[d - 1], recv.at[d - 1], device)
            out.start()
            waits.append(out)
            incoming.append(
                remote(src_to(target), dst_from(source), send.at[d - 1], recv.at[d - 1], device)
            )

        def wait():
            for copy in incoming:
                copy.wait_recv()

        return wait

    starts = [jnp.int32(0)]
    for k in range(r.scene_lengths.shape[0] - 1):
        starts.append(starts[-1] + r.scene_lengths[k])

    def segment(position):
        found = (position >= starts[0]).astype(i32)
        for s in starts[1:]:
            found = found + (position >= s).astype(i32)
        return found

    first_token = seq * T

    def norm_rows(i, _):
        rows = pl.ds(pl.multiple_of(i * ROWS, ROWS), ROWS)
        x = r.block_input[rows, :].astype(f32)
        inverse = lax.rsqrt(jnp.mean(x * x, axis=1, keepdims=True) + epsilon)
        r.inverse[rows, :] = jnp.broadcast_to(inverse, (ROWS, LANES))
        r.normed[rows, :] = (x * inverse * r.input_gain[...].reshape(1, D)).astype(bf)
        return 0

    lax.fori_loop(0, T // ROWS, norm_rows, 0)

    stage("projections")
    r.misc_weight[...] = jnp.zeros_like(r.misc_weight)
    r.misc_weight[0:NS, :] = r.state_weight[...]
    r.misc_weight[NS : NS + H, :] = r.step_weight[...]
    normed_all = r.normed[...]
    for j in range(HI // 256):
        cols = slice(256 * j, 256 * j + 256)
        value = dg(normed_all, r.inner_weight[:, cols], 1, 0)
        r.inner_ext[2 * j, PAD : PAD + T, :] = value[:, :LANES]
        r.inner_ext[2 * j + 1, PAD : PAD + T, :] = value[:, LANES:]
    r.misc_ext[0, PAD : PAD + T, :] = dg(normed_all, r.misc_weight[...], 1, 1)

    stage("barrier")
    pl.semaphore_wait(barrier, n_seq - 1 + n_tp - 1)
    stage("gate_projection")
    right = ((seq + 1) % n_seq, tp)
    left = ((seq + n_seq - 1) % n_seq, tp)
    rim = [
        remote(
            ref.at[:, pl.ds(T, PAD)],
            ref.at[:, pl.ds(0, PAD)],
            r.rim_send.at[k],
            r.rim_recv.at[k],
            right,
        )
        for k, ref in enumerate((r.inner_ext, r.misc_ext))
    ]
    for copy in rim:
        copy.start()
    waits.extend(rim)
    for j in range(HI // 256):
        cols = slice(256 * j, 256 * j + 256)
        r.gate_pre[:, cols] = dg(normed_all, r.gate_weight[:, cols], 1, 0)

    stage("convolutions")
    def agreements(base, rows):
        position = first_token + base + iota((rows, LANES), 0)
        now = segment(position)
        return [segment(position - (CONV - 1) + k) == now for k in range(CONV - 1)]

    def conv_block(ext, taps, bias, base, lanes, masks):
        value = bias[:, lanes]
        for k in range(CONV):
            window = ext[pl.ds(base + PAD - CONV + 1 + k, ROWS), :]
            term = taps[k : k + 1, lanes] * window
            value = value + (term if k == CONV - 1 else jnp.where(masks[k], term, 0.0))
        return value

    r.misc_taps[...] = jnp.zeros_like(r.misc_taps)
    r.misc_taps[0:CONV, 0:NS] = r.state_kernel[...]
    r.misc_taps[CONV : CONV + 1, 0:NS] = r.state_conv_bias[...].reshape(1, NS)
    r.inner_bias[...] = r.inner_conv_bias[...].reshape(1, HI)
    stage("rim_wait")
    for copy in rim:
        copy.wait_recv()
    stage("conv")

    def misc_conv_rows(i, _):
        base = pl.multiple_of(i * ROWS, ROWS)
        masks = agreements(base, ROWS)
        taps = r.misc_taps[...]
        value = conv_block(
            r.misc_ext.at[0], taps, taps[CONV : CONV + 1], base, slice(0, LANES), masks
        )
        r.misc_conv[pl.ds(base, ROWS), :] = value
        return 0

    lax.fori_loop(0, T // ROWS, misc_conv_rows, 0)
    low_lanes = iota((T // 2, LANES), 1) < NS
    own = r.misc_conv[...]
    own = own * jax.nn.sigmoid(own)
    r.state_send[...] = jnp.where(
        low_lanes, own[: T // 2], pltpu.roll(own[T // 2 :], NS, 1)
    ).astype(bf)
    r.state_recv[tp] = r.state_send[...]
    state_wait = spread(
        "tp",
        lambda t: r.state_send,
        lambda t: r.state_recv.at[t],
        r.state_ss,
        r.state_rs,
    )

    def inner_conv_rows(i, _):
        base = pl.multiple_of(i * ROWS, ROWS)
        rows = pl.ds(base, ROWS)
        masks = agreements(base, ROWS)
        taps = r.inner_kernel[...]
        for g in range(NP):
            lanes = slice(g * LANES, g * LANES + LANES)
            value = conv_block(r.inner_ext.at[g], taps, r.inner_bias, base, lanes, masks)
            r.inner_conv[rows, lanes] = value
            r.act[rows, lanes] = (value * jax.nn.sigmoid(value)).astype(bf)
        return 0

    lax.fori_loop(0, T // ROWS, inner_conv_rows, 0)

    stage("decays")
    eye = iota((H, H), 0) == iota((H, H), 1)

    def column(ref):
        wide = jnp.broadcast_to(ref[...].reshape(1, H), (H, H))
        return jnp.sum(jnp.where(eye, wide, 0.0), axis=1, keepdims=True)

    step_in = r.misc_ext[0, PAD : PAD + T, :].T[NS : NS + H, :] + column(r.step_bias)
    step = jnp.maximum(step_in, 0.0) + jnp.log1p(jnp.exp(-jnp.abs(step_in)))
    rate = jnp.exp(column(r.rate_log))
    log_decay = step * -rate
    r.sigmoid_step[...] = jax.nn.sigmoid(step_in)
    r.log_decay[...] = log_decay
    r.step_rows[...] = step
    r.upto[...] = (iota((Q, Q), 0) <= iota((Q, Q), 1)).astype(f32).astype(bf)
    r.expand[...] = (iota((3 * H, HI), 0) % H == iota((3 * H, HI), 1) // P_).astype(f32).astype(bf)
    expand = r.expand[...]

    entering, tailing, chunk_decay = [], [], []
    ones_rows = jnp.ones((1, Q), f32)
    for c in range(NC):
        cols = slice(c * Q, c * Q + Q)
        cumulative = fold3(dg(split3(log_decay[:, cols]), r.upto[...], 1, 0))
        start = first_token + c * Q
        seg_row = segment(start + iota((H, Q), 1))
        seg_before = segment(start - 1)
        seg_end = segment(start + Q - 1)
        last = cumulative[:, Q - 1 : Q]
        enter = jnp.where(seg_row == seg_before, jnp.exp(cumulative), 0.0)
        tail = jnp.where(seg_row == seg_end, jnp.exp(last - cumulative), 0.0)
        entering.append(enter)
        tailing.append(tail)
        chunk_decay.append(enter[:, Q - 1 : Q])
        seg_col = segment(start + iota((Q, Q), 0))
        seg_lane = segment(start + iota((Q, Q), 1))
        keep = (seg_col == seg_lane) & (iota((Q, Q), 0) >= iota((Q, Q), 1))
        r.mask[c] = jnp.where(keep, 0.0, -1e30)
        high = cumulative.astype(bf).astype(f32)
        middle = (cumulative - high).astype(bf).astype(f32)
        rest = cumulative - high - middle
        which = iota((16, Q), 0)
        for h in range(H):
            parts = jnp.where(
                which % 3 == 0,
                high[h : h + 1],
                jnp.where(which % 3 == 1, middle[h : h + 1], rest[h : h + 1]),
            )
            first = which < 3
            second = (which >= 3) & (which < 6)
            r.cum_left[h, :, cols] = jnp.where(
                first, parts, jnp.where(second, 1.0, 0.0)
            ).astype(bf)
            r.cum_right[h, :, cols] = jnp.where(
                first, 1.0, jnp.where(second, -parts, 0.0)
            ).astype(bf)

    def wide(v):
        return dg(split3(v), expand, 0, 0)

    def wide_rows(v):
        return dg(expand, split3(jnp.broadcast_to(v, (H, LANES))), 0, 0)

    for c in range(NC):
        rows = slice(c * Q, c * Q + Q)
        r.step_wide[rows, :] = wide(step[:, rows])
        r.enter_wide[rows, :] = wide(entering[c])
        r.tail_wide[rows, :] = wide(tailing[c])
        r.decay_wide[c] = wide_rows(chunk_decay[c])
    r.skip_wide[...] = dg(split3(jnp.broadcast_to(column(r.skip_scale), (H, 8))), expand, 0, 0)

    def scaled_rows(i, _):
        rows = pl.ds(pl.multiple_of(i * ROWS, ROWS), ROWS)
        x = r.act[rows, :].astype(f32)
        r.xt[rows, :], r.xt_rest[rows, :] = halves(x * r.step_wide[rows, :] * r.tail_wide[rows, :])
        return 0

    lax.fori_loop(0, T // ROWS, scaled_rows, 0)

    stage("keys_wait")
    state_wait()
    shards = n_tp // 2
    half_low = iota((T // 2, LANES), 1) < NS
    for ref, at in ((r.keys, 0), (r.queries, shards)):
        one, two = r.state_recv[at].astype(f32), r.state_recv[at + 1].astype(f32)
        ref[0 : T // 2, :] = jnp.where(half_low, one, pltpu.roll(two, NS, 1)).astype(bf)
        ref[T // 2 : T, :] = jnp.where(half_low, pltpu.roll(one, NS, 1), two).astype(bf)

    stage("end_states")
    end_state = None
    device_decay = None
    for c in range(NC):
        rows = slice(c * Q, c * Q + Q)
        keys = r.keys[rows, :]
        fresh = dg(r.xt[rows, :], keys, 0, 0) + dg(r.xt_rest[rows, :], keys, 0, 0)
        r.fresh[c] = fresh
        end_state = fresh if c == 0 else r.decay_wide[c] * end_state + fresh
        device_decay = chunk_decay[c] if c == 0 else device_decay * chunk_decay[c]
    r.end_send[...] = end_state
    r.decay_send[...] = jnp.broadcast_to(device_decay, (H, LANES))

    def block(ref, device):
        return ref.at[pl.ds(pl.multiple_of(device * R, R), R)]

    r.end_recv[seq] = r.end_send[pl.ds(pl.multiple_of(seq * R, R), R), :]
    r.decay_recv[seq] = r.decay_send[...]
    decay_wait = spread(
        "seq", lambda d: r.decay_send, lambda d: r.decay_recv.at[d], r.decay_ss, r.decay_rs
    )
    end_wait = spread(
        "seq", lambda d: block(r.end_send, d), lambda d: r.end_recv.at[d], r.end_ss, r.end_rs
    )

    stage("inside")
    for c in range(NC):
        rows = slice(c * Q, c * Q + Q)
        r.scores[c] = dg(r.queries[rows, :], r.keys[rows, :], 1, 1)
    low = iota((Q, LANES), 1) < P_

    def inside(i, _):
        c = i // NP
        p = i % NP
        rows = pl.ds(pl.multiple_of(c * Q, Q), Q)
        lanes = pl.ds(pl.multiple_of(p * LANES, LANES), LANES)
        x = r.act[rows, lanes]
        zero = jnp.zeros_like(x)
        result = None
        for s in range(2):
            h = 2 * p + s
            difference = dg(r.cum_left[h, :, rows], r.cum_right[h, :, rows], 0, 0)
            decay = jnp.exp(difference + r.mask[c])
            r.decays[c, h] = decay
            weight, rest = halves(decay * r.scores[c] * r.step_rows[pl.ds(h, 1), rows])
            part = jnp.where(low, x, zero) if s == 0 else jnp.where(low, zero, x)
            term = dg(weight, part, 1, 0) + dg(rest, part, 1, 0)
            result = term if s == 0 else result + term
        r.mixed[rows, lanes] = result
        return 0

    lax.fori_loop(0, NC * NP, inside, 0)
    for j in range(HI // 256):
        cols = slice(256 * j, 256 * j + 256)
        r.norm_grad[:, cols] = dg(r.out_cotangent[...], r.out_weight[cols, :], 1, 1)

    stage("entering")
    head_of = (seq * R) // P_
    stage("end_wait")
    end_wait()
    decay_wait()

    def decay_of(d):
        return jnp.broadcast_to(r.decay_recv[d, pl.ds(head_of, 1), :], (R, LANES))

    running = jnp.zeros((R, N), f32)
    for d in range(n_seq):
        r.enter_send[d] = running
        running = decay_of(d) * running + r.end_recv[d]
    own_rows = pl.ds(pl.multiple_of(seq * R, R), R)
    r.enter_state[own_rows, :] = r.enter_send[seq]
    enter_wait = spread(
        "seq", lambda d: r.enter_send.at[d], lambda d: block(r.enter_state, d), r.enter_ss, r.enter_rs
    )
    stage("enter_wait")
    enter_wait()
    stage("readout")
    for c in range(NC):
        rows = slice(c * Q, c * Q + Q)
        if c == 0:
            state = r.enter_state[...]
        else:
            state = r.decay_wide[c - 1] * state + r.fresh[c - 1]
        r.state_in[c] = state
        r.state_in_low[c], r.state_in_rest[c] = halves(state)
        for j in range(HI // 256):
            cols = slice(256 * j, 256 * j + 256)
            queries = r.queries[rows, :]
            read = dg(queries, r.state_in_low[c, cols, :], 1, 1) + dg(queries, r.state_in_rest[c, cols, :], 1, 1)
            r.mixed[rows, cols] = r.mixed[rows, cols] + r.enter_wide[rows, cols] * read

    stage("gated")
    skip_row = r.skip_wide[0:1, :]
    r.gain_row[...] = r.gate_gain[...].reshape(1, HI)

    def gated_rows(i, _):
        rows = pl.ds(pl.multiple_of(i * ROWS, ROWS), ROWS)
        heads = r.mixed[rows, :] + skip_row * r.act[rows, :].astype(f32)
        gate = r.gate_pre[rows, :]
        gated = heads * (gate * jax.nn.sigmoid(gate))
        r.heads_out[rows, :] = heads
        r.gated[rows, :] = gated
        scaled = r.norm_grad[rows, :] * r.gain_row[...]
        squares = gated * gated
        products = scaled * gated

        def lane_sum(v):
            total = v[:, :LANES]
            for g in range(1, NP):
                total = total + v[:, g * LANES : g * LANES + LANES]
            return total

        r.squares[rows, :] = lane_sum(squares)
        r.products[rows, :] = lane_sum(products)
        return 0

    lax.fori_loop(0, T // ROWS, gated_rows, 0)
    square_row = jnp.sum(r.squares[...].T, axis=0, keepdims=True)
    product_row = jnp.sum(r.products[...].T, axis=0, keepdims=True)
    r.sums_send[...] = jnp.where(
        iota((8, T), 0) == 0,
        jnp.broadcast_to(square_row, (8, T)),
        jnp.broadcast_to(product_row, (8, T)),
    )
    r.sums_recv[tp] = r.sums_send[...]
    sums_wait = spread(
        "tp", lambda t: r.sums_send, lambda t: r.sums_recv.at[t], r.sums_ss, r.sums_rs
    )
    stage("sums_wait")
    sums_wait()
    stage("sums")
    sums = r.sums_recv[0]
    for t in range(1, n_tp):
        sums = sums + r.sums_recv[t]
    count = HI * n_tp
    norm_row = lax.rsqrt(sums[0:1] / count + epsilon)
    back_row = norm_row * norm_row * norm_row * (sums[1:2] / count)
    r.norm_col[...] = jnp.broadcast_to(norm_row, (LANES, T)).T
    r.back_col[...] = jnp.broadcast_to(back_row, (LANES, T)).T

    stage("back_gated")
    r.head_sum[...] = (iota((HI, LANES), 0) // P_ == iota((HI, LANES), 1)).astype(f32).astype(bf)
    r.sum_acc[...] = jnp.zeros_like(r.sum_acc)

    def tile4(v):
        return jnp.concatenate([v] * NP, axis=1)

    def summed(v, which):
        high, lowv = halves(v)
        return dg(high, which, 1, 0) + dg(lowv, which, 1, 0)

    def back_rows(i, _):
        rows = pl.ds(pl.multiple_of(i * ROWS, ROWS), ROWS)
        norm = tile4(r.norm_col[rows, :])
        back = tile4(r.back_col[rows, :])
        gated = r.gated[rows, :]
        grad = r.norm_grad[rows, :]
        gain = r.gain_row[...]
        gate = r.gate_pre[rows, :]
        sigma = jax.nn.sigmoid(gate)
        unit = gated * norm
        r.gated_norm[rows, :] = (unit * gain).astype(bf)
        r.sum_acc[0] = r.sum_acc[0] + fold8(grad * unit)
        gated_grad = norm * (grad * gain) - gated * back
        heads_grad = gated_grad * (gate * sigma)
        heads = r.heads_out[rows, :]
        r.gate_grad[rows, :] = (
            gated_grad * heads * (sigma * (1.0 + gate * (1.0 - sigma)))
        ).astype(bf)
        r.heads_grad[rows, :] = heads_grad
        x = r.act[rows, :].astype(f32)
        r.sum_acc[1] = r.sum_acc[1] + fold8(heads_grad * x)
        r.dy[rows, :], r.dy_rest[rows, :] = halves(heads_grad)
        r.dy_enter[rows, :], r.dy_enter_rest[rows, :] = halves(heads_grad * r.enter_wide[rows, :])
        r.sum_y[rows, :] = summed(heads_grad * r.mixed[rows, :], r.head_sum[...])
        return 0

    lax.fori_loop(0, T // ROWS, back_rows, 0)

    stage("grad_states")
    grad_in = None
    for c in reversed(range(NC)):
        rows = slice(c * Q, c * Q + Q)
        queries = r.queries[rows, :]
        local = dg(r.dy_enter[rows, :], queries, 0, 0) + dg(r.dy_enter_rest[rows, :], queries, 0, 0)
        r.grad_local[c] = local
        grad_in = local if grad_in is None else r.decay_wide[c] * grad_in + local
    r.grad_send[...] = grad_in
    r.grad_recv[seq] = r.grad_send[own_rows, :]
    grad_wait = spread(
        "seq", lambda d: block(r.grad_send, d), lambda d: r.grad_recv.at[d], r.grad_ss, r.grad_rs
    )
    for j in range(D // 256):
        cols = slice(256 * j, 256 * j + 256)
        r.branch[:, cols] = dg(r.gated_norm[...], r.out_weight[:, cols], 1, 0).astype(bf)

    r.score_grad[...] = jnp.zeros_like(r.score_grad)

    def inside_back(i, _):
        c = i // NP
        p = i % NP
        rows = pl.ds(pl.multiple_of(c * Q, Q), Q)
        lanes = pl.ds(pl.multiple_of(p * LANES, LANES), LANES)
        x = r.act[rows, lanes]
        dy = r.dy[rows, lanes]
        dy_rest = r.dy_rest[rows, lanes]
        zero = jnp.zeros_like(dy)
        result = None
        for s in range(2):
            h = 2 * p + s
            decay = r.decays[c, h]
            weight, rest = halves(decay * r.scores[c])

            def masked(v):
                return jnp.where(low, v, zero) if s == 0 else jnp.where(low, zero, v)

            part, part_rest = masked(dy), masked(dy_rest)
            pairs = dg(part, x, 1, 1) + dg(part_rest, x, 1, 1)
            r.score_grad[c] = r.score_grad[c] + pairs * (decay * r.step_rows[pl.ds(h, 1), rows])
            term = dg(weight, part, 0, 0) + dg(rest, part, 0, 0) + dg(weight, part_rest, 0, 0)
            result = term if s == 0 else result + term
        r.x_inside[rows, lanes] = result
        return 0

    lax.fori_loop(0, NC * NP, inside_back, 0)

    stage("grad_wait")
    grad_wait()
    stage("leave_scan")
    running = jnp.zeros((R, N), f32)
    for d in reversed(range(n_seq)):
        r.leave_send[d] = running
        running = decay_of(d) * running + r.grad_recv[d]
    r.leave_grad[own_rows, :] = r.leave_send[seq]
    leave_wait = spread(
        "seq", lambda d: r.leave_send.at[d], lambda d: block(r.leave_grad, d), r.leave_ss, r.leave_rs
    )

    stage("weights_one")
    def weight_rows(i, _):
        cols = pl.ds(pl.multiple_of(i * LANES, LANES), LANES)
        r.wg_one[cols, 0:HI] = dg(r.normed[:, cols], r.gate_grad[...], 0, 0).astype(bf)
        r.wg_one[cols, HI : 2 * HI] = dg(r.out_cotangent[:, cols], r.gated_norm[...], 0, 0).astype(bf)
        return 0

    lax.fori_loop(0, D // LANES, weight_rows, 0)

    def part_of(ref, device):
        return ref.at[pl.ds(pl.multiple_of(device * R2, R2), R2)]

    mine = pl.ds(pl.multiple_of(seq * R2, R2), R2)
    r.wg_one_recv[seq] = r.wg_one[mine, :]
    wg_one_wait = spread(
        "seq", lambda d: part_of(r.wg_one, d), lambda d: r.wg_one_recv.at[d], r.wg1_ss, r.wg1_rs
    )

    stage("leave_wait")
    leave_wait()
    stage("leave")
    carry_terms = [None] * NC
    for c in reversed(range(NC)):
        rows = slice(c * Q, c * Q + Q)
        if c == NC - 1:
            grad = r.leave_grad[...]
        else:
            grad = r.decay_wide[c + 1] * grad + r.grad_local[c + 1]
        grad_low, grad_rest = halves(grad)
        keys, queries = r.keys[rows, :], r.queries[rows, :]
        for j in range(HI // 256):
            cols = slice(256 * j, 256 * j + 256)
            read = dg(keys, grad_low[cols, :], 1, 1) + dg(keys, grad_rest[cols, :], 1, 1)
            r.x_carry[rows, cols] = r.tail_wide[rows, cols] * read
        high, lowv = halves(grad * r.state_in[c])
        pair = dg(expand[0:H], high, 1, 0) + dg(expand[0:H], lowv, 1, 0)
        carry_terms[c] = chunk_decay[c] * jnp.sum(pair, axis=1, keepdims=True)
        score_low, score_rest = halves(r.score_grad[c])
        r.query_grad[rows, :] = (
            dg(score_low, keys, 1, 0)
            + dg(score_rest, keys, 1, 0)
            + dg(r.dy_enter[rows, :], r.state_in_low[c], 1, 0)
            + dg(r.dy_enter_rest[rows, :], r.state_in_low[c], 1, 0)
            + dg(r.dy_enter[rows, :], r.state_in_rest[c], 1, 0)
        )
        r.key_grad[rows, :] = (
            dg(score_low, queries, 0, 0)
            + dg(score_rest, queries, 0, 0)
            + dg(r.xt[rows, :], grad_low, 1, 0)
            + dg(r.xt_rest[rows, :], grad_low, 1, 0)
            + dg(r.xt[rows, :], grad_rest, 1, 0)
        )

    stage("shared")
    for k, ref in enumerate((r.key_grad, r.query_grad)):
        top, bottom = ref[0 : T // 2, :], ref[T // 2 : T, :]
        r.shared_send[k * shards] = jnp.where(half_low, top, pltpu.roll(bottom, NS, 1))
        r.shared_send[k * shards + 1] = jnp.where(half_low, pltpu.roll(top, NS, 1), bottom)
    r.shared_recv[tp] = r.shared_send[tp]
    shared_wait = spread(
        "tp", lambda t: r.shared_send.at[t], lambda t: r.shared_recv.at[t], r.shared_ss, r.shared_rs
    )

    stage("x_grads")
    r.head_sum_two[...] = (
        iota((HI, LANES), 0) // P_ + H == iota((HI, LANES), 1)
    ).astype(f32).astype(bf)
    r.head_sum_three[...] = (
        iota((HI, LANES), 0) // P_ + 2 * H == iota((HI, LANES), 1)
    ).astype(f32).astype(bf)

    def x_rows(i, _):
        rows = pl.ds(pl.multiple_of(i * ROWS, ROWS), ROWS)
        x = r.act[rows, :].astype(f32)
        z = r.x_inside[rows, :]
        carried = r.x_carry[rows, :]
        both = z + carried
        step_rows = r.step_wide[rows, :]
        xs = x * step_rows
        x_grad = step_rows * both + skip_row * r.heads_grad[rows, :]
        conv_grad = x_grad * slope(r.inner_conv[rows, :])
        for g in range(NP):
            r.grad_ext[g, rows, :] = conv_grad[:, g * LANES : g * LANES + LANES]
        r.sum_x[rows, :] = (
            summed(x * both, r.head_sum[...])
            + summed(xs * carried, r.head_sum_two[...])
            + summed(xs * z, r.head_sum_three[...])
        )
        return 0

    lax.fori_loop(0, T // ROWS, x_rows, 0)
    halo_one = remote(
        r.grad_ext.at[:, pl.ds(0, PAD)],
        r.grad_ext.at[:, pl.ds(T, PAD)],
        r.halo_send.at[0],
        r.halo_recv.at[0],
        left,
    )
    halo_one.start()
    waits.append(halo_one)

    sums_y = r.sum_y[...].T
    sums_x = r.sum_x[...].T
    step_grad = sums_x[0:H]
    tail_part = sums_x[H : 2 * H]
    pair_part = sums_y[0:H] - sums_x[2 * H : 3 * H]
    decay_grads = []
    for c in range(NC):
        cols = slice(c * Q, c * Q + Q)
        suffix = fold3(dg(split3(pair_part[:, cols]), r.upto[...], 1, 1))
        before = fold3(dg(split3(tail_part[:, cols]), r.upto[...], 1, 0)) - tail_part[:, cols]
        decay_grads.append(suffix + before + carry_terms[c])
    decay_grad = jnp.concatenate(decay_grads, axis=1)
    step_total = step_grad - rate * decay_grad
    step_pre_grad = step_total * r.sigmoid_step[...]
    rate_sum = jnp.sum(r.log_decay[...] * decay_grad, axis=1, keepdims=True)
    bias_sum = jnp.sum(step_pre_grad, axis=1, keepdims=True)
    step_cols = jnp.concatenate(
        [jnp.zeros((NS, T), f32), step_pre_grad, jnp.zeros((LANES - NS - H, T), f32)], axis=0
    ).T

    stage("conv_back")
    def after_masks(base):
        position = first_token + base + iota((ROWS, LANES), 0)
        now = segment(position)
        masks = []
        for k in range(CONV - 1):
            later = position + (CONV - 1) - k
            masks.append((segment(later) == now) & (later < total_tokens))
        return masks

    def conv_back(ext, taps, base, lanes, masks):
        value = None
        for k in range(CONV):
            term = taps[k : k + 1, lanes] * ext[pl.ds(base + CONV - 1 - k, ROWS), :]
            if k < CONV - 1:
                term = jnp.where(masks[k], term, 0.0)
            value = term if value is None else value + term
        return value

    def tap_sums(ext, grad, base, masks):
        sums = []
        for k in range(CONV):
            term = grad * ext[pl.ds(base + PAD - CONV + 1 + k, ROWS), :]
            sums.append(fold8(term if k == CONV - 1 else jnp.where(masks[k], term, 0.0)))
        return sums + [fold8(grad)]

    stage("halo_one_wait")
    halo_one.wait_recv()
    stage("inner_back")

    def inner_back_rows(i, _):
        base = pl.multiple_of(i * ROWS, ROWS)
        rows = pl.ds(base, ROWS)
        masks = after_masks(base)
        before = agreements(base, ROWS)
        taps = r.inner_kernel[...]
        for g in range(NP):
            lanes = slice(g * LANES, g * LANES + LANES)
            r.inner_grad[rows, lanes] = conv_back(r.grad_ext.at[g], taps, base, lanes, masks).astype(bf)
            found = tap_sums(r.inner_ext.at[g], r.grad_ext[g, rows, :], base, before)
            for k, v in enumerate(found):
                r.sum_acc[2 + k, :, lanes] = r.sum_acc[2 + k, :, lanes] + v
        return 0

    lax.fori_loop(0, T // ROWS, inner_back_rows, 0)

    stage("shared_wait")
    shared_wait()
    stage("shared_use")
    packed = r.shared_recv[0]
    for t in range(1, n_tp):
        packed = packed + r.shared_recv[t]
    r.state_grad_ext[0 : T // 2, :] = packed * slope(r.misc_conv[0 : T // 2, :])
    r.state_grad_ext[T // 2 : T, :] = pltpu.roll(packed, NS, 1) * slope(r.misc_conv[T // 2 : T, :])
    halo_two = remote(
        r.state_grad_ext.at[pl.ds(0, PAD)],
        r.state_grad_ext.at[pl.ds(T, PAD)],
        r.halo_send.at[1],
        r.halo_recv.at[1],
        left,
    )
    halo_two.start()
    waits.append(halo_two)
    stage("halo_two_wait")
    halo_two.wait_recv()
    stage("misc_back")
    r.misc_acc[...] = jnp.zeros_like(r.misc_acc)
    r.step_cols[...] = step_cols

    def misc_back_rows(i, _):
        base = pl.multiple_of(i * ROWS, ROWS)
        rows = pl.ds(base, ROWS)
        masks = after_masks(base)
        before = agreements(base, ROWS)
        taps = r.misc_taps[...]
        lanes = slice(0, LANES)
        value = conv_back(r.state_grad_ext, taps, base, lanes, masks)
        value = jnp.where(iota((ROWS, LANES), 1) < NS, value, r.step_cols[rows, :])
        r.misc_grad[rows, :] = value.astype(bf)
        found = tap_sums(r.misc_ext.at[0], r.state_grad_ext[rows, :], base, before)
        for k, v in enumerate(found):
            r.misc_acc[k] = r.misc_acc[k] + v
        return 0

    lax.fori_loop(0, T // ROWS, misc_back_rows, 0)

    stage("normed_grad")
    for j in range(D // 256):
        cols = slice(256 * j, 256 * j + 256)
        value = (
            dg(r.gate_grad[...], r.gate_weight[cols, :], 1, 1)
            + dg(r.inner_grad[...], r.inner_weight[cols, :], 1, 1)
            + dg(r.misc_grad[...], r.misc_weight[:, cols], 1, 0)
        )
        r.normed_part[:, cols] = value.astype(bf)
        hats = r.block_input[:, cols].astype(f32) * jnp.concatenate([r.inverse[...]] * 2, axis=1)
        r.gain_part[:, cols] = fold8(value * hats)

    def weight_rows_two(i, _):
        cols = pl.ds(pl.multiple_of(i * LANES, LANES), LANES)
        r.wg_two[cols, 0:HI] = dg(r.normed[:, cols], r.inner_grad[...], 0, 0).astype(bf)
        r.wg_two[cols, HI : HI + LANES] = dg(r.normed[:, cols], r.misc_grad[...], 0, 0).astype(bf)
        return 0

    lax.fori_loop(0, D // LANES, weight_rows_two, 0)
    r.wg_two_recv[seq] = r.wg_two[mine, :]
    wg_two_wait = spread(
        "seq", lambda d: part_of(r.wg_two, d), lambda d: r.wg_two_recv.at[d], r.wg2_ss, r.wg2_rs
    )

    stage("small_sums")
    def row_of(v):
        return jnp.sum(v, axis=0, keepdims=True)

    eye_wide = iota((H, LANES), 0) == iota((H, LANES), 1)

    def lanes_of(v):
        return row_of(jnp.where(eye_wide, jnp.broadcast_to(v, (H, LANES)), 0.0))

    r.small_send[...] = jnp.zeros_like(r.small_send)
    for k in range(CONV + 1):
        r.small_send[k : k + 1, :] = row_of(r.sum_acc[2 + k])
    r.small_send[5:6, :] = row_of(r.sum_acc[0])
    r.small_send[6:7, :] = row_of(r.sum_acc[1])
    for k in range(CONV):
        r.small_send[7:8, k * LANES : k * LANES + LANES] = row_of(r.misc_acc[k])
    r.small_send[8:9, 0:LANES] = row_of(r.misc_acc[CONV])
    r.small_send[8:9, LANES : 2 * LANES] = lanes_of(bias_sum)
    r.small_send[8:9, 2 * LANES : 3 * LANES] = lanes_of(rate_sum)
    gain_rows = row_of(r.gain_part[...])
    for k in range(D // HI):
        r.small_send[9 + k : 10 + k, :] = gain_rows[:, k * HI : k * HI + HI]
    r.small_recv[seq] = r.small_send[...]
    small_wait = spread(
        "seq", lambda d: r.small_send, lambda d: r.small_recv.at[d], r.small_ss, r.small_rs
    )
    stage("small_wait")
    small_wait()
    stage("small_use")
    total = r.small_recv[0]
    for d in range(1, n_seq):
        total = total + r.small_recv[d]
    r.small_total[...] = total
    r.gain_recv[tp] = r.small_total[8:16, :]
    gain_wait = spread(
        "tp", lambda t: r.small_total.at[pl.ds(8, 8)], lambda t: r.gain_recv.at[t], r.gain_ss, r.gain_rs
    )

    stage("chains")
    pieces = r.chain_ss.shape[2]
    piece = T // (2 * pieces)
    summed_refs = ((r.branch, r.branch_hop, r.branch_sum), (r.normed_part, r.normed_hop, r.normed_sum))

    def chain_for(k):
        events = []
        for a in range(2):
            for j in range(pieces):
                for way in range(2):
                    place = k if way == 0 else n_tp - 1 - k
                    at = a * pieces + j
                    events.append((at + place * 1.0, 0, a, j, way, place))
                    if place < n_tp - 1:
                        events.append((at + (n_tp - 1) + (n_tp - 1 - place) + 0.5, 1, a, j, way, place))
        for _, back, a, j, way, place in sorted(events):
            partial, hop, final = summed_refs[a]
            rows = pl.ds((way * pieces + j) * piece, piece)
            on = (seq, k + 1) if way == 0 else (seq, k - 1)
            home = (seq, k - 1) if way == 0 else (seq, k + 1)
            sems = (a, way, j)

            def go(src, dst, send, recv, device):
                return remote(src.at[rows], dst.at[rows], send.at[sems], recv.at[sems], device)

            if not back:
                if place > 0:
                    go(hop, hop, r.chain_ss, r.chain_rs, home).wait_recv()
                    both = (partial[rows, :].astype(f32) + hop[rows, :].astype(f32)).astype(bf)
                    if place == n_tp - 1:
                        final[rows, :] = both
                    else:
                        partial[rows, :] = both
                if place < n_tp - 1:
                    go(partial, hop, r.chain_ss, r.chain_rs, on).start()
                else:
                    go(final, final, r.back_ss, r.back_rs, home).start()
            else:
                go(final, final, r.back_ss, r.back_rs, on).wait_recv()
                if place > 0:
                    go(final, final, r.back_ss, r.back_rs, home).start()
        for _, back, a, j, way, place in sorted(events):
            partial, hop, final = summed_refs[a]
            rows = pl.ds((way * pieces + j) * piece, piece)
            sems = (a, way, j)
            on = (seq, k + 1) if way == 0 else (seq, k - 1)
            home = (seq, k - 1) if way == 0 else (seq, k + 1)
            if not back:
                if place < n_tp - 1:
                    remote(partial.at[rows], hop.at[rows], r.chain_ss.at[sems], r.chain_rs.at[sems], on).wait_send()
                if place > 0:
                    remote(final.at[rows], final.at[rows], r.back_ss.at[sems], r.back_rs.at[sems], home).wait_send()

    for k in range(n_tp):
        pl.when(tp == k)(functools.partial(chain_for, k))

    stage("weights_wait")
    wg_one_wait()
    wg_two_wait()
    gain_wait()
    stage("weight_sums")

    def weight_sums(ref, recv):
        value = recv[0].astype(f32)
        for d in range(1, n_seq):
            value = value + recv[d].astype(f32)
        ref[...] = value

    weight_sums(r.sum_one, r.wg_one_recv)
    weight_sums(r.sum_two, r.wg_two_recv)
    gains = r.gain_recv[0]
    for t in range(1, n_tp):
        gains = gains + r.gain_recv[t]
    r.gain_total[...] = gains
    stage("drain")
    for copy in waits:
        copy.wait_send()
    marks.close()


def finish(sizes, names, *refs):
    r = types.SimpleNamespace(**dict(zip(names, refs)))
    T, D, HI, H, NS = sizes
    P_ = HI // H

    def final_rows(i, _):
        rows = pl.ds(pl.multiple_of(i * ROWS, ROWS), ROWS)
        x = r.block_input[rows, :].astype(f32)
        r.block_output[rows, :] = (x + r.branch_sum[rows, :].astype(f32)).astype(bf)
        inverse = lax.rsqrt(jnp.mean(x * x, axis=1, keepdims=True) + epsilon)
        hat = x * inverse
        hat_grad = r.normed_sum[rows, :].astype(f32) * r.input_gain[...].reshape(1, D)
        mean = jnp.mean(hat_grad * hat, axis=1, keepdims=True)
        r.input_grad[rows, :] = r.out_cotangent[rows, :].astype(f32) + inverse * (
            hat_grad - hat * mean
        )
        return 0

    lax.fori_loop(0, T // ROWS, final_rows, 0)
    r.gate_weight_grad[...] = r.sum_one[:, 0:HI]
    r.out_weight_grad[...] = r.sum_one[:, HI : 2 * HI].T
    r.inner_weight_grad[...] = r.sum_two[:, 0:HI]
    narrow = r.sum_two[:, HI : HI + LANES].T
    r.state_weight_grad[...] = narrow[0:NS]
    r.step_weight_grad[...] = narrow[NS : NS + H]
    small = r.small_total
    r.inner_kernel_grad[...] = small[0:CONV, :]
    r.inner_conv_bias_grad[...] = small[CONV : CONV + 1, :].reshape(HI)
    r.gate_gain_grad[...] = small[5:6, :].reshape(HI)
    head_sum = (iota((HI, LANES), 0) // P_ == iota((HI, LANES), 1)).astype(f32).astype(bf)
    skip_sums = fold3(dg(split3(jnp.broadcast_to(small[6:7, :], (8, HI))), head_sum, 1, 0))
    r.skip_scale_grad[...] = skip_sums[0:1, 0:H].reshape(H)
    for k in range(CONV):
        r.state_kernel_grad[k : k + 1, :] = small[7:8, k * LANES : k * LANES + NS]
    r.state_conv_bias_grad[...] = small[8:9, 0:NS].reshape(NS)
    r.step_bias_grad[...] = small[8:9, LANES : LANES + H].reshape(H)
    r.rate_log_grad[...] = small[8:9, 2 * LANES : 2 * LANES + H].reshape(H)
    for k in range(D // HI):
        r.input_gain_grad[k * HI : k * HI + HI] = r.gain_total[1 + k : 2 + k, :].reshape(HI)


INPUTS = (
    "block_input",
    "scene_lengths",
    "input_gain",
    "gate_weight",
    "inner_weight",
    "state_weight",
    "step_weight",
    "step_bias",
    "rate_log",
    "inner_kernel",
    "inner_conv_bias",
    "state_kernel",
    "state_conv_bias",
    "skip_scale",
    "gate_gain",
    "out_weight",
    "out_cotangent",
)
OUTPUTS = (
    "block_output",
    "input_grad",
    "input_gain_grad",
    "gate_weight_grad",
    "inner_weight_grad",
    "state_weight_grad",
    "step_weight_grad",
    "step_bias_grad",
    "rate_log_grad",
    "inner_kernel_grad",
    "inner_conv_bias_grad",
    "state_kernel_grad",
    "state_conv_bias_grad",
    "skip_scale_grad",
    "gate_gain_grad",
    "out_weight_grad",
)


SUMS = ("branch_sum", "normed_sum", "sum_one", "sum_two", "small_total", "gain_total")


def local(*args):
    given = dict(zip(INPUTS, args))
    given["state_weight"] = given["state_weight"].T
    given["step_weight"] = given["step_weight"].T
    n_seq = lax.axis_size("seq")
    n_tp = lax.axis_size("tp")
    T, D = given["block_input"].shape
    HI = given["gate_weight"].shape[1]
    H = given["step_bias"].shape[0]
    NS = given["state_weight"].shape[0]
    N = STATE
    Q = CHUNK
    NC = T // Q
    NP = HI // LANES
    R = HI // n_seq
    R2 = D // n_seq
    pieces = 4
    outs = (
        ((T, D), bf),
        ((T, D), f32),
        ((D,), f32),
        ((R2, HI), f32),
        ((R2, HI), f32),
        ((NS, R2), f32),
        ((H, R2), f32),
        ((H,), f32),
        ((H,), f32),
        ((CONV, HI), f32),
        ((HI,), f32),
        ((CONV, NS), f32),
        ((NS,), f32),
        ((H,), f32),
        ((HI,), f32),
        ((HI, R2), f32),
    )
    sums = (
        ((T, D), bf),
        ((T, D), bf),
        ((R2, 2 * HI), f32),
        ((R2, HI + LANES), f32),
        ((16, HI), f32),
        ((8, HI), f32),
    )
    scratch = dict(
        inverse=((T, LANES), f32),
        normed=((T, D), bf),
        misc_weight=((LANES, D), bf),
        inner_ext=((NP, T + PAD, LANES), f32),
        misc_ext=((1, T + PAD, LANES), f32),
        gate_pre=((T, HI), f32),
        misc_taps=((8, LANES), f32),
        inner_bias=((1, HI), f32),
        gain_row=((1, HI), f32),
        misc_conv=((T, LANES), f32),
        inner_conv=((T, HI), f32),
        act=((T, HI), bf),
        state_send=((T // 2, LANES), bf),
        state_recv=((n_tp, T // 2, LANES), bf),
        keys=((T, N), bf),
        queries=((T, N), bf),
        sigmoid_step=((H, T), f32),
        step_rows=((H, T), f32),
        log_decay=((H, T), f32),
        upto=((Q, Q), bf),
        expand=((3 * H, HI), bf),
        mask=((NC, Q, Q), f32),
        cum_left=((H, 16, T), bf),
        cum_right=((H, 16, T), bf),
        step_wide=((T, HI), f32),
        enter_wide=((T, HI), f32),
        tail_wide=((T, HI), f32),
        decay_wide=((NC, HI, LANES), f32),
        skip_wide=((8, HI), f32),
        xt=((T, HI), bf),
        xt_rest=((T, HI), bf),
        fresh=((NC, HI, N), f32),
        end_send=((HI, N), f32),
        end_recv=((n_seq, R, N), f32),
        decay_send=((H, LANES), f32),
        decay_recv=((n_seq, H, LANES), f32),
        enter_send=((n_seq, R, N), f32),
        enter_state=((HI, N), f32),
        state_in=((NC, HI, N), f32),
        state_in_low=((NC, HI, N), bf),
        state_in_rest=((NC, HI, N), bf),
        scores=((NC, Q, Q), f32),
        score_grad=((NC, Q, Q), f32),
        decays=((NC, H, Q, Q), f32),
        mixed=((T, HI), f32),
        norm_grad=((T, HI), f32),
        heads_out=((T, HI), f32),
        gated=((T, HI), f32),
        squares=((T, LANES), f32),
        products=((T, LANES), f32),
        sums_send=((8, T), f32),
        sums_recv=((n_tp, 8, T), f32),
        norm_col=((T, LANES), f32),
        back_col=((T, LANES), f32),
        head_sum=((HI, LANES), bf),
        head_sum_two=((HI, LANES), bf),
        head_sum_three=((HI, LANES), bf),
        sum_acc=((7, 8, HI), f32),
        gated_norm=((T, HI), bf),
        gate_grad=((T, HI), bf),
        heads_grad=((T, HI), f32),
        dy=((T, HI), bf),
        dy_rest=((T, HI), bf),
        dy_enter=((T, HI), bf),
        dy_enter_rest=((T, HI), bf),
        sum_y=((T, LANES), f32),
        sum_x=((T, LANES), f32),
        grad_local=((NC, HI, N), f32),
        grad_send=((HI, N), f32),
        grad_recv=((n_seq, R, N), f32),
        leave_send=((n_seq, R, N), f32),
        leave_grad=((HI, N), f32),
        x_inside=((T, HI), f32),
        x_carry=((T, HI), f32),
        wg_one=((D, 2 * HI), bf),
        wg_one_recv=((n_seq, R2, 2 * HI), bf),
        wg_two=((D, HI + LANES), bf),
        wg_two_recv=((n_seq, R2, HI + LANES), bf),
        query_grad=((T, N), f32),
        key_grad=((T, N), f32),
        shared_send=((n_tp, T // 2, LANES), f32),
        shared_recv=((n_tp, T // 2, LANES), f32),
        grad_ext=((NP, T + PAD, LANES), f32),
        state_grad_ext=((T + PAD, LANES), f32),
        inner_grad=((T, HI), bf),
        step_cols=((T, LANES), f32),
        misc_grad=((T, LANES), bf),
        misc_acc=((CONV + 1, 8, LANES), f32),
        normed_part=((T, D), bf),
        normed_hop=((T, D), bf),
        branch=((T, D), bf),
        branch_hop=((T, D), bf),
        gain_part=((8, D), f32),
        small_send=((16, HI), f32),
        small_recv=((n_seq, 16, HI), f32),
        gain_recv=((n_tp, 8, HI), f32),
    )
    semaphores = dict(
        rim_send=(2,),
        rim_recv=(2,),
        halo_send=(2,),
        halo_recv=(2,),
        chain_ss=(2, 2, pieces),
        chain_rs=(2, 2, pieces),
        back_ss=(2, 2, pieces),
        back_rs=(2, 2, pieces),
    )
    for name in ("state", "sums", "shared", "gain"):
        semaphores[name + "_ss"] = (n_tp - 1,)
        semaphores[name + "_rs"] = (n_tp - 1,)
    for name in ("decay", "end", "enter", "grad", "leave", "wg1", "wg2", "small"):
        semaphores[name + "_ss"] = (n_seq - 1,)
        semaphores[name + "_rs"] = (n_seq - 1,)
    names = INPUTS + SUMS + tuple(scratch) + tuple(semaphores)
    vmem = pl.BlockSpec(memory_space=pltpu.VMEM)
    smem = pl.BlockSpec(memory_space=pltpu.SMEM)
    totals = pl.pallas_call(
        functools.partial(kernel, (n_seq, n_tp, T, D, HI, H, NS), names),
        out_shape=tuple(jax.ShapeDtypeStruct(s, t) for s, t in sums),
        in_specs=[smem if n == "scene_lengths" else vmem for n in INPUTS],
        out_specs=tuple(vmem for _ in sums),
        scratch_shapes=[pltpu.VMEM(s, t) for s, t in scratch.values()]
        + [pltpu.SemaphoreType.DMA(s) for s in semaphores.values()],
        compiler_params=pltpu.CompilerParams(
            collective_id=0, has_side_effects=True, vmem_limit_bytes=60 * 2**20
        ),
    )(*given.values())
    needed = ("block_input", "input_gain", "out_cotangent")
    results = pl.pallas_call(
        functools.partial(finish, (T, D, HI, H, NS), needed + SUMS + OUTPUTS),
        out_shape=tuple(jax.ShapeDtypeStruct(s, t) for s, t in outs),
        in_specs=[vmem] * (len(needed) + len(SUMS)),
        out_specs=tuple(vmem for _ in outs),
        compiler_params=pltpu.CompilerParams(vmem_limit_bytes=32 * 2**20),
    )(*(given[n] for n in needed), *totals)
    results = dict(zip(OUTPUTS, results))
    results["state_weight_grad"] = results["state_weight_grad"].T
    results["step_weight_grad"] = results["step_weight_grad"].T
    return tuple(results.values())


def solution(mesh):
    rows = P("seq", None)
    cols = P(None, "tp")
    heads = P("tp")
    return jax.shard_map(
        local,
        mesh=mesh,
        in_specs=(
            rows,
            P(),
            P(),
            cols,
            cols,
            cols,
            cols,
            heads,
            heads,
            cols,
            heads,
            cols,
            heads,
            heads,
            heads,
            P("tp", None),
            rows,
        ),
        out_specs=(
            rows,
            rows,
            P(),
            P("seq", "tp"),
            P("seq", "tp"),
            P("seq", "tp"),
            P("seq", "tp"),
            heads,
            heads,
            cols,
            heads,
            cols,
            heads,
            heads,
            heads,
            P("tp", "seq"),
        ),
        check_vma=False,
    )
```

profile of v0, /device:TPU:0, one launch (start us, length us, event | category | flops | bytes accessed | tf_op | source)
XLA Modules:
  0.0 177.4 jit_solution(12942542513060497517)
XLA Ops:
  0.7 0.0 copy-start
  0.7 0.0 copy-start.1
  0.7 0.0 copy-start.8
  0.7 166.7 %shard_map.288 = (bf16[512,1024]{1,0:T(8,128)(2,1)}, bf16[512,1024]{1,0:T(8,128)(2,1)}, f32[128,1024]{1,0:T(8,128)}, f32[128,640]{1,0:T(8,128)}, f32[16,512]{1,0:T(8,128)}, /*index=5*/f32[8,512]{1,0:T(8,128)}) custom-call(bf16[512,1024]{1,0:T(8,128)(2,1)} %refs_0_.3, s32[4]{0:T(128)} %refs_1_.2, f32[1024]{0:T(1024)} %refs_1_.3, bf16[1024,512]{1,0:T(8,128)(2,1)} %refs_3_.1, ...), custom_call_target="tpu_custom_call" | custom-call | tf_op jit(solution)/shard_map/pallas_call | solution.py:1163
  167.4 0.0 copy-done
  167.4 0.0 copy-done.1
  167.5 0.0 copy-done.8
  167.5 0.0 copy-start.2
  167.5 1.2 copy-done.2
  168.7 0.0 copy-start.3
  168.7 1.2 copy-done.3
  169.9 0.0 copy-start.4
  169.9 1.0 copy-done.4
  171.0 0.0 copy-start.5
  171.0 1.0 copy-done.5
  171.9 0.0 copy-start.6
  171.9 0.8 copy-done.6
  172.7 0.0 copy-start.7
  172.7 0.7 copy-done.7
  173.4 3.8 %shard_map.289 = (bf16[512,1024]{1,0:T(8,128)(2,1)}, f32[512,1024]{1,0:T(8,128)}, f32[1024]{0:T(1024)}, f32[128,512]{1,0:T(8,128)}, f32[128,512]{1,0:T(8,128)}, ...) custom-call(bf16[512,1024]{1,0:T(8,128)(2,1)S(1)} %copy-done, ...), custom_call_target="tpu_custom_call" | custom-call | tf_op jit(solution)/shard_map/pallas_call | solution.py:1175
Async XLA Ops:
  0.7 166.8 %copy-start = (bf16[512,1024]{1,0:T(8,128)(2,1)S(1)}, bf16[512,1024]{1,0:T(8,128)(2,1)}, u32[]{:S(2)}) copy-start(bf16[512,1024]{1,0:T(8,128)(2,1)} %refs_0_.3) | copy-start | bytes 3145732
  0.7 166.8 %copy-start.1 = (bf16[512,1024]{1,0:T(8,128)(2,1)S(1)}, bf16[512,1024]{1,0:T(8,128)(2,1)}, u32[]{:S(2)}) copy-start(bf16[512,1024]{1,0:T(8,128)(2,1)} %refs_2_.3) | copy-start | bytes 3145732
  0.7 166.8 %copy-start.8 = (f32[1024]{0:T(1024)S(1)}, f32[1024]{0:T(1024)}, u32[]{:S(2)}) copy-start(f32[1024]{0:T(1024)} %refs_1_.3) | copy-start | bytes 12292
  167.5 1.2 copy-start.2
  168.7 1.2 copy-start.3
  169.9 1.0 copy-start.4
  171.0 1.0 copy-start.5
  171.9 0.8 copy-start.6
  172.7 0.7 copy-start.7
where the time goes:
time: 178 us; the launch traced here: 177 us
  Pallas kernels  171 us (96%)
  local copies, waits for them, and re-layouts  5.94 us (3%)
    pallas_call x1, Pallas kernels, local(): pl.pallas_call(functools.partial(kernel, (n_seq, n_tp, T, D, HI, H, NS),...  167 us
    unnamed x18, local copies, waits for them, and re-layouts  5.94 us
    pallas_call x1, Pallas kernels, local(): pl.pallas_call(functools.partial(finish, (T, D, HI, H, NS), needed + SUMS...  3.83 us

commit v1 on v0

--- a/solution.py
+++ b/solution.py
@@ -85,6 +85,64 @@
         )
 
     waits = []
+    half = n_tp // 2
+    inner = jnp.where(tp < half, tp + 1, tp - 1)
+    outer = jnp.where(tp < half, tp - 1, tp + 1)
+    is_middle = (tp == half - 1) | (tp == half)
+    has_outer = (tp > 0) & (tp < n_tp - 1)
+    fold_pieces = (r.branch_in.shape[0], r.normed_in.shape[0])
+    fold_width = tuple(D // n for n in fold_pieces)
+    fold_refs = (
+        (r.branch, r.branch_in, r.branch_across, r.branch_sum),
+        (r.normed_part, r.normed_in, r.normed_across, r.normed_sum),
+    )
+
+    def fold(a, j):
+        partial, arrived, across, total = (
+            ref.at[j] if k < 3 else ref.at[:, pl.ds(j * fold_width[a], fold_width[a])]
+            for k, ref in enumerate(fold_refs[a])
+        )
+        return partial, arrived, across, total
+
+    def fold_copy(a, j, leg):
+        partial, arrived, across, total = fold(a, j)
+        sems = leg, sum(fold_pieces[:a]) + j
+        source, target, place = ((partial, arrived, inner), (partial, across, inner), (total, total, outer))[leg]
+        return remote(source, target, r.fold_ss.at[sems], r.fold_rs.at[sems], (seq, place))
+
+    def fold_start(a, j):
+        pl.when(jnp.logical_not(has_outer | is_middle))(fold_copy(a, j, 0).start)
+
+    def fold_in(a, j):
+        partial, arrived, _, _ = fold(a, j)
+
+        @pl.when(has_outer)
+        def _():
+            fold_copy(a, j, 0).wait_recv()
+            partial[...] = (partial[...].astype(f32) + arrived[...].astype(f32)).astype(bf)
+
+        pl.when(is_middle)(fold_copy(a, j, 1).start)
+        pl.when(has_outer & jnp.logical_not(is_middle))(fold_copy(a, j, 0).start)
+
+    def fold_middle(a, j):
+        partial, _, across, total = fold(a, j)
+
+        @pl.when(is_middle)
+        def _():
+            fold_copy(a, j, 1).wait_recv()
+            total[...] = (partial[...].astype(f32) + across[...].astype(f32)).astype(bf)
+            pl.when(has_outer)(fold_copy(a, j, 2).start)
+
+    def fold_end(a, j):
+        @pl.when(jnp.logical_not(is_middle))
+        def _():
+            fold_copy(a, j, 2).wait_recv()
+            pl.when(has_outer)(fold_copy(a, j, 2).start)
+            fold_copy(a, j, 0).wait_send()
+
+        pl.when(has_outer)(fold_copy(a, j, 2).wait_send)
+        pl.when(is_middle)(fold_copy(a, j, 1).wait_send)
+
     marks = contextlib.ExitStack()
 
     def stage(name):
@@ -522,10 +580,12 @@
     grad_wait = spread(
         "seq", lambda d: block(r.grad_send, d), lambda d: r.grad_recv.at[d], r.grad_ss, r.grad_rs
     )
-    for j in range(D // 256):
-        cols = slice(256 * j, 256 * j + 256)
-        r.branch[:, cols] = dg(r.gated_norm[...], r.out_weight[:, cols], 1, 0).astype(bf)
-
+    stage("out_projection")
+    for j in range(fold_pieces[0]):
+        cols = slice(fold_width[0] * j, fold_width[0] * (j + 1))
+        r.branch[j] = dg(r.gated_norm[...], r.out_weight[:, cols], 1, 0).astype(bf)
+        fold_start(0, j)
+    stage("inside_back")
     r.score_grad[...] = jnp.zeros_like(r.score_grad)
 
     def inside_back(i, _):
@@ -556,6 +616,37 @@
 
     lax.fori_loop(0, NC * NP, inside_back, 0)
 
+    stage("query_grad")
+    for c in range(NC):
+        rows = slice(c * Q, c * Q + Q)
+        score_low = r.score_grad[c].astype(bf)
+        r.query_grad[rows, :] = (
+            dg(score_low, r.keys[rows, :], 1, 0)
+            + dg(r.dy_enter[rows, :], r.state_in_low[c], 1, 0)
+            + dg(r.dy_enter_rest[rows, :], r.state_in_low[c], 1, 0)
+            + dg(r.dy_enter[rows, :], r.state_in_rest[c], 1, 0)
+        )
+
+    def shared_copy(d, arriving=False):
+        target = (tp + d) % n_tp
+        slot = (tp + n_tp - d) % n_tp if arriving else tp
+        sems = (r.shared_ss.at[d - 1], r.shared_rs.at[d - 1])
+        return remote(r.shared_send.at[target], r.shared_recv.at[slot], *sems, (seq, target))
+
+    def pack_shared(ref, group):
+        top, bottom = ref[0 : T // 2, :], ref[T // 2 : T, :]
+        at = group * shards
+        r.shared_send[at] = jnp.where(half_low, top, pltpu.roll(bottom, NS, 1)).astype(bf)
+        r.shared_send[at + 1] = jnp.where(half_low, pltpu.roll(top, NS, 1), bottom).astype(bf)
+
+        @pl.when(tp // shards == group)
+        def _():
+            r.shared_recv[tp] = r.shared_send[tp]
+
+        for d in range(1, n_tp):
+            pl.when((tp + d) % n_tp // shards == group)(shared_copy(d).start)
+
+    pack_shared(r.query_grad, 1)
     stage("grad_wait")
     grad_wait()
     stage("leave_scan")
@@ -577,6 +668,12 @@
 
     lax.fori_loop(0, D // LANES, weight_rows, 0)
 
+    stage("poll_one")
+    fold_in(0, 0)
+    fold_in(0, 1)
+    stage("leave_wait")
+    leave_wait()
+    stage("leave")
     def part_of(ref, device):
         return ref.at[pl.ds(pl.multiple_of(device * R2, R2), R2)]
 
@@ -586,9 +683,6 @@
         "seq", lambda d: part_of(r.wg_one, d), lambda d: r.wg_one_recv.at[d], r.wg1_ss, r.wg1_rs
     )
 
-    stage("leave_wait")
-    leave_wait()
-    stage("leave")
     carry_terms = [None] * NC
     for c in reversed(range(NC)):
         rows = slice(c * Q, c * Q + Q)
@@ -605,32 +699,15 @@
         high, lowv = halves(grad * r.state_in[c])
         pair = dg(expand[0:H], high, 1, 0) + dg(expand[0:H], lowv, 1, 0)
         carry_terms[c] = chunk_decay[c] * jnp.sum(pair, axis=1, keepdims=True)
-        score_low, score_rest = halves(r.score_grad[c])
-        r.query_grad[rows, :] = (
-            dg(score_low, keys, 1, 0)
-            + dg(score_rest, keys, 1, 0)
-            + dg(r.dy_enter[rows, :], r.state_in_low[c], 1, 0)
-            + dg(r.dy_enter_rest[rows, :], r.state_in_low[c], 1, 0)
-            + dg(r.dy_enter[rows, :], r.state_in_rest[c], 1, 0)
-        )
+        score_low = r.score_grad[c].astype(bf)
         r.key_grad[rows, :] = (
             dg(score_low, queries, 0, 0)
-            + dg(score_rest, queries, 0, 0)
             + dg(r.xt[rows, :], grad_low, 1, 0)
             + dg(r.xt_rest[rows, :], grad_low, 1, 0)
             + dg(r.xt[rows, :], grad_rest, 1, 0)
         )
 
-    stage("shared")
-    for k, ref in enumerate((r.key_grad, r.query_grad)):
-        top, bottom = ref[0 : T // 2, :], ref[T // 2 : T, :]
-        r.shared_send[k * shards] = jnp.where(half_low, top, pltpu.roll(bottom, NS, 1))
-        r.shared_send[k * shards + 1] = jnp.where(half_low, pltpu.roll(top, NS, 1), bottom)
-    r.shared_recv[tp] = r.shared_send[tp]
-    shared_wait = spread(
-        "tp", lambda t: r.shared_send.at[t], lambda t: r.shared_recv.at[t], r.shared_ss, r.shared_rs
-    )
-
+    pack_shared(r.key_grad, 0)
     stage("x_grads")
     r.head_sum_two[...] = (
         iota((HI, LANES), 0) // P_ + H == iota((HI, LANES), 1)
@@ -715,6 +792,9 @@
             sums.append(fold8(term if k == CONV - 1 else jnp.where(masks[k], term, 0.0)))
         return sums + [fold8(grad)]
 
+    stage("poll_two")
+    fold_in(0, 2)
+    fold_middle(0, 0)
     stage("halo_one_wait")
     halo_one.wait_recv()
     stage("inner_back")
@@ -735,12 +815,16 @@
 
     lax.fori_loop(0, T // ROWS, inner_back_rows, 0)
 
+    stage("poll_three")
+    fold_in(0, 3)
+    fold_middle(0, 1)
     stage("shared_wait")
-    shared_wait()
+    for d in range(1, n_tp):
+        shared_copy(d, True).wait_recv()
     stage("shared_use")
-    packed = r.shared_recv[0]
+    packed = r.shared_recv[0].astype(f32)
     for t in range(1, n_tp):
-        packed = packed + r.shared_recv[t]
+        packed = packed + r.shared_recv[t].astype(f32)
     r.state_grad_ext[0 : T // 2, :] = packed * slope(r.misc_conv[0 : T // 2, :])
     r.state_grad_ext[T // 2 : T, :] = pltpu.roll(packed, NS, 1) * slope(r.misc_conv[T // 2 : T, :])
     halo_two = remote(
@@ -776,30 +860,23 @@
     lax.fori_loop(0, T // ROWS, misc_back_rows, 0)
 
     stage("normed_grad")
-    for j in range(D // 256):
-        cols = slice(256 * j, 256 * j + 256)
+    width = fold_width[1]
+    for j in range(fold_pieces[1]):
+        cols = slice(width * j, width * (j + 1))
         value = (
             dg(r.gate_grad[...], r.gate_weight[cols, :], 1, 1)
             + dg(r.inner_grad[...], r.inner_weight[cols, :], 1, 1)
             + dg(r.misc_grad[...], r.misc_weight[:, cols], 1, 0)
         )
-        r.normed_part[:, cols] = value.astype(bf)
-        hats = r.block_input[:, cols].astype(f32) * jnp.concatenate([r.inverse[...]] * 2, axis=1)
+        r.normed_part[j] = value.astype(bf)
+        fold_start(1, j)
+        hats = r.block_input[:, cols].astype(f32) * jnp.concatenate(
+            [r.inverse[...]] * (width // LANES), axis=1
+        )
         r.gain_part[:, cols] = fold8(value * hats)
 
-    def weight_rows_two(i, _):
-        cols = pl.ds(pl.multiple_of(i * LANES, LANES), LANES)
-        r.wg_two[cols, 0:HI] = dg(r.normed[:, cols], r.inner_grad[...], 0, 0).astype(bf)
-        r.wg_two[cols, HI : HI + LANES] = dg(r.normed[:, cols], r.misc_grad[...], 0, 0).astype(bf)
-        return 0
-
-    lax.fori_loop(0, D // LANES, weight_rows_two, 0)
-    r.wg_two_recv[seq] = r.wg_two[mine, :]
-    wg_two_wait = spread(
-        "seq", lambda d: part_of(r.wg_two, d), lambda d: r.wg_two_recv.at[d], r.wg2_ss, r.wg2_rs
-    )
-
     stage("small_sums")
+
     def row_of(v):
         return jnp.sum(v, axis=0, keepdims=True)
 
@@ -825,9 +902,24 @@
     small_wait = spread(
         "seq", lambda d: r.small_send, lambda d: r.small_recv.at[d], r.small_ss, r.small_rs
     )
+    stage("poll_four")
+    fold_middle(0, 2)
+    fold_middle(0, 3)
+    stage("weights_two")
+
+    def weight_rows_two(i, _):
+        cols = pl.ds(pl.multiple_of(i * LANES, LANES), LANES)
+        r.wg_two[cols, 0:HI] = dg(r.normed[:, cols], r.inner_grad[...], 0, 0).astype(bf)
+        r.wg_two[cols, HI : HI + LANES] = dg(r.normed[:, cols], r.misc_grad[...], 0, 0).astype(bf)
+        return 0
+
+    lax.fori_loop(0, D // LANES, weight_rows_two, 0)
+    r.wg_two_recv[seq] = r.wg_two[mine, :]
+    wg_two_wait = spread(
+        "seq", lambda d: part_of(r.wg_two, d), lambda d: r.wg_two_recv.at[d], r.wg2_ss, r.wg2_rs
+    )
     stage("small_wait")
     small_wait()
-    stage("small_use")
     total = r.small_recv[0]
     for d in range(1, n_seq):
         total = total + r.small_recv[d]
@@ -837,61 +929,16 @@
         "tp", lambda t: r.small_total.at[pl.ds(8, 8)], lambda t: r.gain_recv.at[t], r.gain_ss, r.gain_rs
     )
 
-    stage("chains")
-    pieces = r.chain_ss.shape[2]
-    piece = T // (2 * pieces)
-    summed_refs = ((r.branch, r.branch_hop, r.branch_sum), (r.normed_part, r.normed_hop, r.normed_sum))
-
-    def chain_for(k):
-        events = []
-        for a in range(2):
-            for j in range(pieces):
-                for way in range(2):
-                    place = k if way == 0 else n_tp - 1 - k
-                    at = a * pieces + j
-                    events.append((at + place * 1.0, 0, a, j, way, place))
-                    if place < n_tp - 1:
-                        events.append((at + (n_tp - 1) + (n_tp - 1 - place) + 0.5, 1, a, j, way, place))
-        for _, back, a, j, way, place in sorted(events):
-            partial, hop, final = summed_refs[a]
-            rows = pl.ds((way * pieces + j) * piece, piece)
-            on = (seq, k + 1) if way == 0 else (seq, k - 1)
-            home = (seq, k - 1) if way == 0 else (seq, k + 1)
-            sems = (a, way, j)
-
-            def go(src, dst, send, recv, device):
-                return remote(src.at[rows], dst.at[rows], send.at[sems], recv.at[sems], device)
-
-            if not back:
-                if place > 0:
-                    go(hop, hop, r.chain_ss, r.chain_rs, home).wait_recv()
-                    both = (partial[rows, :].astype(f32) + hop[rows, :].astype(f32)).astype(bf)
-                    if place == n_tp - 1:
-                        final[rows, :] = both
-                    else:
-                        partial[rows, :] = both
-                if place < n_tp - 1:
-                    go(partial, hop, r.chain_ss, r.chain_rs, on).start()
-                else:
-                    go(final, final, r.back_ss, r.back_rs, home).start()
-            else:
-                go(final, final, r.back_ss, r.back_rs, on).wait_recv()
-                if place > 0:
-                    go(final, final, r.back_ss, r.back_rs, home).start()
-        for _, back, a, j, way, place in sorted(events):
-            partial, hop, final = summed_refs[a]
-            rows = pl.ds((way * pieces + j) * piece, piece)
-            sems = (a, way, j)
-            on = (seq, k + 1) if way == 0 else (seq, k - 1)
-            home = (seq, k - 1) if way == 0 else (seq, k + 1)
-            if not back:
-                if place < n_tp - 1:
-                    remote(partial.at[rows], hop.at[rows], r.chain_ss.at[sems], r.chain_rs.at[sems], on).wait_send()
-                if place > 0:
-                    remote(final.at[rows], final.at[rows], r.back_ss.at[sems], r.back_rs.at[sems], home).wait_send()
-
-    for k in range(n_tp):
-        pl.when(tp == k)(functools.partial(chain_for, k))
+    stage("folds")
+    for j in range(fold_pieces[1] + 1):
+        if j < fold_pieces[1]:
+            fold_in(1, j)
+        if j > 0:
+            fold_middle(1, j - 1)
+    for j in range(fold_pieces[0]):
+        fold_end(0, j)
+    for j in range(fold_pieces[1]):
+        fold_end(1, j)
 
     stage("weights_wait")
     wg_one_wait()
@@ -912,6 +959,8 @@
         gains = gains + r.gain_recv[t]
     r.gain_total[...] = gains
     stage("drain")
+    for d in range(1, n_tp):
+        shared_copy(d).wait_send()
     for copy in waits:
         copy.wait_send()
     marks.close()
@@ -1016,7 +1065,6 @@
     NP = HI // LANES
     R = HI // n_seq
     R2 = D // n_seq
-    pieces = 4
     outs = (
         ((T, D), bf),
         ((T, D), f32),
@@ -1124,18 +1172,20 @@
         wg_two_recv=((n_seq, R2, HI + LANES), bf),
         query_grad=((T, N), f32),
         key_grad=((T, N), f32),
-        shared_send=((n_tp, T // 2, LANES), f32),
-        shared_recv=((n_tp, T // 2, LANES), f32),
+        shared_send=((n_tp, T // 2, LANES), bf),
+        shared_recv=((n_tp, T // 2, LANES), bf),
         grad_ext=((NP, T + PAD, LANES), f32),
         state_grad_ext=((T + PAD, LANES), f32),
         inner_grad=((T, HI), bf),
         step_cols=((T, LANES), f32),
         misc_grad=((T, LANES), bf),
         misc_acc=((CONV + 1, 8, LANES), f32),
-        normed_part=((T, D), bf),
-        normed_hop=((T, D), bf),
-        branch=((T, D), bf),
-        branch_hop=((T, D), bf),
+        normed_part=((8, T, D // 8), bf),
+        normed_in=((8, T, D // 8), bf),
+        normed_across=((8, T, D // 8), bf),
+        branch=((4, T, D // 4), bf),
+        branch_in=((4, T, D // 4), bf),
+        branch_across=((4, T, D // 4), bf),
         gain_part=((8, D), f32),
         small_send=((16, HI), f32),
         small_recv=((n_seq, 16, HI), f32),
@@ -1146,10 +1196,8 @@
         rim_recv=(2,),
         halo_send=(2,),
         halo_recv=(2,),
-        chain_ss=(2, 2, pieces),
-        chain_rs=(2, 2, pieces),
-        back_ss=(2, 2, pieces),
-        back_rs=(2, 2, pieces),
+        fold_ss=(3, 12),
+        fold_rs=(3, 12),
     )
     for name in ("state", "sums", "shared", "gain"):
         semaphores[name + "_ss"] = (n_tp - 1,)
@@ -1177,7 +1225,7 @@
         out_shape=tuple(jax.ShapeDtypeStruct(s, t) for s, t in outs),
         in_specs=[vmem] * (len(needed) + len(SUMS)),
         out_specs=tuple(vmem for _ in outs),
-        compiler_params=pltpu.CompilerParams(vmem_limit_bytes=32 * 2**20),
+        compiler_params=pltpu.CompilerParams(vmem_limit_bytes=60 * 2**20),
     )(*(given[n] for n in needed), *totals)
     results = dict(zip(OUTPUTS, results))
     results["state_weight_grad"] = results["state_weight_grad"].T

time: 178 us -> 130 us (0.73)
  Pallas kernels: 171 us -> 129 us
  local copies, waits for them, and re-layouts: 5.94 us -> 0 us
    pallas_call x1, Pallas kernels: 167 us -> 123 us  [local(): pl.pallas_call(functools.partial(kernel, (n_seq, n_tp, T, D, HI, H, NS),...]
    unnamed x18 -> x0, local copies, waits for them, and re-layouts: 5.94 us -> none
    pallas_call x1, Pallas kernels: 3.83 us -> 6.3 us  [local(): pl.pallas_call(functools.partial(finish, (T, D, HI, H, NS), needed + SUMS...]
where the time goes in v1:
time: 130 us
  Pallas kernels  129 us (99%)
    pallas_call x1, Pallas kernels, local(): pl.pallas_call(functools.partial(kernel, (n_seq, n_tp, T, D, HI, H, NS),...  123 us
    pallas_call x1, Pallas kernels, local(): pl.pallas_call(functools.partial(finish, (T, D, HI, H, NS), needed + SUMS...  6.3 us

profile of v1, /device:TPU:0, one launch (start us, length us, event | category | flops | bytes accessed | tf_op | source)
XLA Modules:
  0.0 129.6 jit_solution(8823098722300276729)
XLA Ops:
  0.7 122.5 %shard_map.288 = (bf16[512,1024]{1,0:T(8,128)(2,1)}, bf16[512,1024]{1,0:T(8,128)(2,1)}, f32[128,1024]{1,0:T(8,128)}, f32[128,640]{1,0:T(8,128)}, f32[16,512]{1,0:T(8,128)}, /*index=5*/f32[8,512]{1,0:T(8,128)}) custom-call(bf16[512,1024]{1,0:T(8,128)(2,1)} %refs_0_.3, s32[4]{0:T(128)} %refs_1_.2, f32[1024]{0:T(1024)} %refs_1_.3, bf16[1024,512]{1,0:T(8,128)(2,1)} %refs_3_.1, ...), custom_call_target="tpu_custom_call" | custom-call | tf_op jit(solution)/shard_map/pallas_call | solution.py:1211
  123.2 6.3 %shard_map.289 = (bf16[512,1024]{1,0:T(8,128)(2,1)}, f32[512,1024]{1,0:T(8,128)}, f32[1024]{0:T(1024)}, f32[128,512]{1,0:T(8,128)}, f32[128,512]{1,0:T(8,128)}, ...) custom-call(bf16[512,1024]{1,0:T(8,128)(2,1)} %refs_0_.3, ...), custom_call_target="tpu_custom_call" | custom-call | tf_op jit(solution)/shard_map/pallas_call | solution.py:1223

commit v2 on v1

--- a/solution.py
+++ b/solution.py
@@ -379,6 +379,18 @@
 
     lax.fori_loop(0, T // ROWS, scaled_rows, 0)
 
+    stage("decay_matrices")
+
+    def decay_matrix(i, _):
+        c = i // H
+        h = i % H
+        rows = pl.ds(pl.multiple_of(c * Q, Q), Q)
+        difference = dg(r.cum_left[h, :, rows], r.cum_right[h, :, rows], 0, 0)
+        r.decays[c, h] = jnp.exp(difference + r.mask[c])
+        return 0
+
+    lax.fori_loop(0, NC * H, decay_matrix, 0)
+
     stage("keys_wait")
     state_wait()
     shards = n_tp // 2
@@ -429,10 +441,7 @@
         result = None
         for s in range(2):
             h = 2 * p + s
-            difference = dg(r.cum_left[h, :, rows], r.cum_right[h, :, rows], 0, 0)
-            decay = jnp.exp(difference + r.mask[c])
-            r.decays[c, h] = decay
-            weight, rest = halves(decay * r.scores[c] * r.step_rows[pl.ds(h, 1), rows])
+            weight, rest = halves(r.decays[c, h] * r.scores[c] * r.step_rows[pl.ds(h, 1), rows])
             part = jnp.where(low, x, zero) if s == 0 else jnp.where(low, zero, x)
             term = dg(weight, part, 1, 0) + dg(rest, part, 1, 0)
             result = term if s == 0 else result + term
@@ -668,21 +677,67 @@
 
     lax.fori_loop(0, D // LANES, weight_rows, 0)
 
+    chips = n_seq // 2
+    core = seq % 2
+    chip = seq // 2
+    sibling = seq + 1 - 2 * core
+
+    def pair_copy(k, q):
+        rows = pl.ds(pl.multiple_of((2 * q + 1 - core) * R2, R2), R2)
+        source, target = ((r.wg_one, r.pair_one), (r.wg_two, r.pair_two))[k]
+        return remote(
+            source.at[rows], target.at[q], r.pair_ss.at[k, q], r.pair_rs.at[k, q], (sibling, tp)
+        )
+
+    def chip_copy(k, d, arriving=False):
+        to = (chip + d) % chips
+        slot = (chip + chips - d) % chips if arriving else chip
+        source, target = ((r.chip_one_send, r.chip_one), (r.chip_two_send, r.chip_two))[k]
+        return remote(
+            source.at[to],
+            target.at[slot],
+            r.chip_ss.at[k, d - 1],
+            r.chip_rs.at[k, d - 1],
+            (2 * to + core, tp),
+        )
+
+    def pair_start(k):
+        for q in range(chips):
+            pair_copy(k, q).start()
+
+    def chip_start(k):
+        own, pair, send, kept = (
+            (r.wg_one, r.pair_one, r.chip_one_send, r.chip_one),
+            (r.wg_two, r.pair_two, r.chip_two_send, r.chip_two),
+        )[k]
+        for q in range(chips):
+            rows = pl.ds(pl.multiple_of((2 * q + core) * R2, R2), R2)
+            pair_copy(k, q).wait_recv()
+            send[q] = (own[rows, :].astype(f32) + pair[q].astype(f32)).astype(bf)
+        for d in range(1, chips):
+            chip_copy(k, d).start()
+        kept[chip] = send[chip]
+
+    def chip_sum(k):
+        kept = (r.chip_one, r.chip_two)[k]
+        for d in range(1, chips):
+            chip_copy(k, d, True).wait_recv()
+        value = kept[0].astype(f32)
+        for q in range(1, chips):
+            value = value + kept[q].astype(f32)
+        for q in range(chips):
+            pair_copy(k, q).wait_send()
+        for d in range(1, chips):
+            chip_copy(k, d).wait_send()
+        return value
+
+    pair_start(0)
     stage("poll_one")
     fold_in(0, 0)
     fold_in(0, 1)
     stage("leave_wait")
     leave_wait()
     stage("leave")
-    def part_of(ref, device):
-        return ref.at[pl.ds(pl.multiple_of(device * R2, R2), R2)]
-
-    mine = pl.ds(pl.multiple_of(seq * R2, R2), R2)
-    r.wg_one_recv[seq] = r.wg_one[mine, :]
-    wg_one_wait = spread(
-        "seq", lambda d: part_of(r.wg_one, d), lambda d: r.wg_one_recv.at[d], r.wg1_ss, r.wg1_rs
-    )
-
     carry_terms = [None] * NC
     for c in reversed(range(NC)):
         rows = slice(c * Q, c * Q + Q)
@@ -708,6 +763,8 @@
         )
 
     pack_shared(r.key_grad, 0)
+    stage("chip_one")
+    chip_start(0)
     stage("x_grads")
     r.head_sum_two[...] = (
         iota((HI, LANES), 0) // P_ + H == iota((HI, LANES), 1)
@@ -792,11 +849,6 @@
             sums.append(fold8(term if k == CONV - 1 else jnp.where(masks[k], term, 0.0)))
         return sums + [fold8(grad)]
 
-    stage("poll_two")
-    fold_in(0, 2)
-    fold_middle(0, 0)
-    stage("halo_one_wait")
-    halo_one.wait_recv()
     stage("inner_back")
 
     def inner_back_rows(i, _):
@@ -813,7 +865,14 @@
                 r.sum_acc[2 + k, :, lanes] = r.sum_acc[2 + k, :, lanes] + v
         return 0
 
-    lax.fori_loop(0, T // ROWS, inner_back_rows, 0)
+    lax.fori_loop(0, T // ROWS - 1, inner_back_rows, 0)
+    stage("poll_two")
+    fold_in(0, 2)
+    fold_middle(0, 0)
+    stage("halo_one_wait")
+    halo_one.wait_recv()
+    stage("inner_back_last")
+    inner_back_rows(T // ROWS - 1, 0)
 
     stage("poll_three")
     fold_in(0, 3)
@@ -836,8 +895,6 @@
     )
     halo_two.start()
     waits.append(halo_two)
-    stage("halo_two_wait")
-    halo_two.wait_recv()
     stage("misc_back")
     r.misc_acc[...] = jnp.zeros_like(r.misc_acc)
     r.step_cols[...] = step_cols
@@ -857,22 +914,26 @@
             r.misc_acc[k] = r.misc_acc[k] + v
         return 0
 
-    lax.fori_loop(0, T // ROWS, misc_back_rows, 0)
+    lax.fori_loop(0, T // ROWS - 1, misc_back_rows, 0)
+    stage("halo_two_wait")
+    halo_two.wait_recv()
+    stage("misc_back_last")
+    misc_back_rows(T // ROWS - 1, 0)
 
     stage("normed_grad")
     width = fold_width[1]
-    for j in range(fold_pieces[1]):
-        cols = slice(width * j, width * (j + 1))
+    for j in range(D // 256):
+        cols = slice(256 * j, 256 * (j + 1))
         value = (
             dg(r.gate_grad[...], r.gate_weight[cols, :], 1, 1)
             + dg(r.inner_grad[...], r.inner_weight[cols, :], 1, 1)
             + dg(r.misc_grad[...], r.misc_weight[:, cols], 1, 0)
         )
-        r.normed_part[j] = value.astype(bf)
-        fold_start(1, j)
-        hats = r.block_input[:, cols].astype(f32) * jnp.concatenate(
-            [r.inverse[...]] * (width // LANES), axis=1
-        )
+        for k in range(256 // width):
+            at = j * (256 // width) + k
+            r.normed_part[at] = value[:, k * width : k * width + width].astype(bf)
+            fold_start(1, at)
+        hats = r.block_input[:, cols].astype(f32) * jnp.concatenate([r.inverse[...]] * 2, axis=1)
         r.gain_part[:, cols] = fold8(value * hats)
 
     stage("small_sums")
@@ -914,50 +975,44 @@
         return 0
 
     lax.fori_loop(0, D // LANES, weight_rows_two, 0)
-    r.wg_two_recv[seq] = r.wg_two[mine, :]
-    wg_two_wait = spread(
-        "seq", lambda d: part_of(r.wg_two, d), lambda d: r.wg_two_recv.at[d], r.wg2_ss, r.wg2_rs
-    )
-    stage("small_wait")
-    small_wait()
-    total = r.small_recv[0]
-    for d in range(1, n_seq):
-        total = total + r.small_recv[d]
-    r.small_total[...] = total
-    r.gain_recv[tp] = r.small_total[8:16, :]
-    gain_wait = spread(
-        "tp", lambda t: r.small_total.at[pl.ds(8, 8)], lambda t: r.gain_recv.at[t], r.gain_ss, r.gain_rs
-    )
-
+    pair_start(1)
     stage("folds")
-    for j in range(fold_pieces[1] + 1):
-        if j < fold_pieces[1]:
+    last = fold_pieces[1]
+    for j in range(last + 1):
+        if j < last:
             fold_in(1, j)
         if j > 0:
             fold_middle(1, j - 1)
+        if j == 0:
+            chip_start(1)
+        if j == 1:
+            small_wait()
+            total = r.small_recv[0]
+            for d in range(1, n_seq):
+                total = total + r.small_recv[d]
+            r.small_total[...] = total
+            r.gain_recv[tp] = r.small_total[8:16, :]
+            gain_wait = spread(
+                "tp",
+                lambda t: r.small_total.at[pl.ds(8, 8)],
+                lambda t: r.gain_recv.at[t],
+                r.gain_ss,
+                r.gain_rs,
+            )
+        if j == last - 1:
+            stage("weight_sums")
+            r.sum_one[...] = chip_sum(0)
+            r.sum_two[...] = chip_sum(1)
+            gain_wait()
+            gains = r.gain_recv[0]
+            for t in range(1, n_tp):
+                gains = gains + r.gain_recv[t]
+            r.gain_total[...] = gains
+            stage("folds_last")
     for j in range(fold_pieces[0]):
         fold_end(0, j)
     for j in range(fold_pieces[1]):
         fold_end(1, j)
-
-    stage("weights_wait")
-    wg_one_wait()
-    wg_two_wait()
-    gain_wait()
-    stage("weight_sums")
-
-    def weight_sums(ref, recv):
-        value = recv[0].astype(f32)
-        for d in range(1, n_seq):
-            value = value + recv[d].astype(f32)
-        ref[...] = value
-
-    weight_sums(r.sum_one, r.wg_one_recv)
-    weight_sums(r.sum_two, r.wg_two_recv)
-    gains = r.gain_recv[0]
-    for t in range(1, n_tp):
-        gains = gains + r.gain_recv[t]
-    r.gain_total[...] = gains
     stage("drain")
     for d in range(1, n_tp):
         shared_copy(d).wait_send()
@@ -970,6 +1025,7 @@
     r = types.SimpleNamespace(**dict(zip(names, refs)))
     T, D, HI, H, NS = sizes
     P_ = HI // H
+    T = r.block_input.shape[0]
 
     def final_rows(i, _):
         rows = pl.ds(pl.multiple_of(i * ROWS, ROWS), ROWS)
@@ -985,26 +1041,28 @@
         return 0
 
     lax.fori_loop(0, T // ROWS, final_rows, 0)
-    r.gate_weight_grad[...] = r.sum_one[:, 0:HI]
-    r.out_weight_grad[...] = r.sum_one[:, HI : 2 * HI].T
-    r.inner_weight_grad[...] = r.sum_two[:, 0:HI]
-    narrow = r.sum_two[:, HI : HI + LANES].T
-    r.state_weight_grad[...] = narrow[0:NS]
-    r.step_weight_grad[...] = narrow[NS : NS + H]
-    small = r.small_total
-    r.inner_kernel_grad[...] = small[0:CONV, :]
-    r.inner_conv_bias_grad[...] = small[CONV : CONV + 1, :].reshape(HI)
-    r.gate_gain_grad[...] = small[5:6, :].reshape(HI)
-    head_sum = (iota((HI, LANES), 0) // P_ == iota((HI, LANES), 1)).astype(f32).astype(bf)
-    skip_sums = fold3(dg(split3(jnp.broadcast_to(small[6:7, :], (8, HI))), head_sum, 1, 0))
-    r.skip_scale_grad[...] = skip_sums[0:1, 0:H].reshape(H)
-    for k in range(CONV):
-        r.state_kernel_grad[k : k + 1, :] = small[7:8, k * LANES : k * LANES + NS]
-    r.state_conv_bias_grad[...] = small[8:9, 0:NS].reshape(NS)
-    r.step_bias_grad[...] = small[8:9, LANES : LANES + H].reshape(H)
-    r.rate_log_grad[...] = small[8:9, 2 * LANES : 2 * LANES + H].reshape(H)
-    for k in range(D // HI):
-        r.input_gain_grad[k * HI : k * HI + HI] = r.gain_total[1 + k : 2 + k, :].reshape(HI)
+    @pl.when(pl.program_id(0) == 0)
+    def _():
+        r.gate_weight_grad[...] = r.sum_one[:, 0:HI]
+        r.out_weight_grad[...] = r.sum_one[:, HI : 2 * HI].T
+        r.inner_weight_grad[...] = r.sum_two[:, 0:HI]
+        narrow = r.sum_two[:, HI : HI + LANES].T
+        r.state_weight_grad[...] = narrow[0:NS]
+        r.step_weight_grad[...] = narrow[NS : NS + H]
+        small = r.small_total
+        r.inner_kernel_grad[...] = small[0:CONV, :]
+        r.inner_conv_bias_grad[...] = small[CONV : CONV + 1, :].reshape(HI)
+        r.gate_gain_grad[...] = small[5:6, :].reshape(HI)
+        head_sum = (iota((HI, LANES), 0) // P_ == iota((HI, LANES), 1)).astype(f32).astype(bf)
+        skip_sums = fold3(dg(split3(jnp.broadcast_to(small[6:7, :], (8, HI))), head_sum, 1, 0))
+        r.skip_scale_grad[...] = skip_sums[0:1, 0:H].reshape(H)
+        for k in range(CONV):
+            r.state_kernel_grad[k : k + 1, :] = small[7:8, k * LANES : k * LANES + NS]
+        r.state_conv_bias_grad[...] = small[8:9, 0:NS].reshape(NS)
+        r.step_bias_grad[...] = small[8:9, LANES : LANES + H].reshape(H)
+        r.rate_log_grad[...] = small[8:9, 2 * LANES : 2 * LANES + H].reshape(H)
+        for k in range(D // HI):
+            r.input_gain_grad[k * HI : k * HI + HI] = r.gain_total[1 + k : 2 + k, :].reshape(HI)
 
 
 INPUTS = (
@@ -1167,9 +1225,13 @@
         x_inside=((T, HI), f32),
         x_carry=((T, HI), f32),
         wg_one=((D, 2 * HI), bf),
-        wg_one_recv=((n_seq, R2, 2 * HI), bf),
+        pair_one=((n_seq // 2, R2, 2 * HI), bf),
+        chip_one_send=((n_seq // 2, R2, 2 * HI), bf),
+        chip_one=((n_seq // 2, R2, 2 * HI), bf),
         wg_two=((D, HI + LANES), bf),
-        wg_two_recv=((n_seq, R2, HI + LANES), bf),
+        pair_two=((n_seq // 2, R2, HI + LANES), bf),
+        chip_two_send=((n_seq // 2, R2, HI + LANES), bf),
+        chip_two=((n_seq // 2, R2, HI + LANES), bf),
         query_grad=((T, N), f32),
         key_grad=((T, N), f32),
         shared_send=((n_tp, T // 2, LANES), bf),
@@ -1196,13 +1258,17 @@
         rim_recv=(2,),
         halo_send=(2,),
         halo_recv=(2,),
+        pair_ss=(2, n_seq // 2),
+        pair_rs=(2, n_seq // 2),
+        chip_ss=(2, n_seq // 2 - 1),
+        chip_rs=(2, n_seq // 2 - 1),
         fold_ss=(3, 12),
         fold_rs=(3, 12),
     )
     for name in ("state", "sums", "shared", "gain"):
         semaphores[name + "_ss"] = (n_tp - 1,)
         semaphores[name + "_rs"] = (n_tp - 1,)
-    for name in ("decay", "end", "enter", "grad", "leave", "wg1", "wg2", "small"):
+    for name in ("decay", "end", "enter", "grad", "leave", "small"):
         semaphores[name + "_ss"] = (n_seq - 1,)
         semaphores[name + "_rs"] = (n_seq - 1,)
     names = INPUTS + SUMS + tuple(scratch) + tuple(semaphores)
@@ -1219,12 +1285,21 @@
             collective_id=0, has_side_effects=True, vmem_limit_bytes=60 * 2**20
         ),
     )(*given.values())
+    tall = ("block_input", "out_cotangent", "branch_sum", "normed_sum", "block_output", "input_grad")
+    steps = 4
+    by_rows = pl.BlockSpec((T // steps, D), lambda i: (i, 0))
+
+    def whole(shape):
+        return pl.BlockSpec(shape, lambda i: (0,) * len(shape))
+
     needed = ("block_input", "input_gain", "out_cotangent")
     results = pl.pallas_call(
         functools.partial(finish, (T, D, HI, H, NS), needed + SUMS + OUTPUTS),
         out_shape=tuple(jax.ShapeDtypeStruct(s, t) for s, t in outs),
-        in_specs=[vmem] * (len(needed) + len(SUMS)),
-        out_specs=tuple(vmem for _ in outs),
+        grid=(steps,),
+        in_specs=[by_rows if n in tall else whole(given[n].shape) for n in needed]
+        + [by_rows if n in tall else whole(s) for n, (s, _) in zip(SUMS, sums)],
+        out_specs=tuple(by_rows if n in tall else whole(s) for n, (s, _) in zip(OUTPUTS, outs)),
         compiler_params=pltpu.CompilerParams(vmem_limit_bytes=60 * 2**20),
     )(*(given[n] for n in needed), *totals)
     results = dict(zip(OUTPUTS, results))

time: 130 us -> 118 us (0.908)
  Pallas kernels: 129 us -> 117 us
    pallas_call x1, Pallas kernels: 123 us -> 111 us  [local(): pl.pallas_call(functools.partial(kernel, (n_seq, n_tp, T, D, HI, H, NS),...]
where the time goes in v2:
time: 118 us
  Pallas kernels  117 us (99%)
    pallas_call x1, Pallas kernels, local(): pl.pallas_call(functools.partial(kernel, (n_seq, n_tp, T, D, HI, H, NS),...  111 us
    pallas_call x1, Pallas kernels, local(): pl.pallas_call(functools.partial(finish, (T, D, HI, H, NS), needed + SUMS...  6.1 us

profile of v2, /device:TPU:0, one launch (start us, length us, event | category | flops | bytes accessed | tf_op | source)
XLA Modules:
  0.0 117.6 jit_solution(2275061898828340462)
XLA Ops:
  0.7 110.7 %shard_map.288 = (bf16[512,1024]{1,0:T(8,128)(2,1)}, bf16[512,1024]{1,0:T(8,128)(2,1)}, f32[128,1024]{1,0:T(8,128)}, f32[128,640]{1,0:T(8,128)}, f32[16,512]{1,0:T(8,128)}, /*index=5*/f32[8,512]{1,0:T(8,128)}) custom-call(bf16[512,1024]{1,0:T(8,128)(2,1)} %refs_0_.3, s32[4]{0:T(128)} %refs_1_.2, f32[1024]{0:T(1024)} %refs_1_.3, bf16[1024,512]{1,0:T(8,128)(2,1)} %refs_3_.1, ...), custom_call_target="tpu_custom_call" | custom-call | tf_op jit(solution)/shard_map/pallas_call | solution.py:1277
  111.3 6.1 %shard_map.289 = (bf16[512,1024]{1,0:T(8,128)(2,1)}, f32[512,1024]{1,0:T(8,128)}, f32[1024]{0:T(1024)}, f32[128,512]{1,0:T(8,128)}, f32[128,512]{1,0:T(8,128)}, ...) custom-call(bf16[512,1024]{1,0:T(8,128)(2,1)} %refs_0_.3, ...), custom_call_target="tpu_custom_call" | custom-call | tf_op jit(solution)/shard_map/pallas_call | solution.py:1296

commit v3 on v2

--- a/solution.py
+++ b/solution.py
@@ -91,15 +91,21 @@
     is_middle = (tp == half - 1) | (tp == half)
     has_outer = (tp > 0) & (tp < n_tp - 1)
     fold_pieces = (r.branch_in.shape[0], r.normed_in.shape[0])
-    fold_width = tuple(D // n for n in fold_pieces)
+    fold_width = D // fold_pieces[0], LANES
+    fold_rows = T, T * D // LANES // fold_pieces[1]
     fold_refs = (
         (r.branch, r.branch_in, r.branch_across, r.branch_sum),
         (r.normed_part, r.normed_in, r.normed_across, r.normed_sum),
     )
 
     def fold(a, j):
+        high = T // fold_rows[a]
+        place = (
+            pl.ds(j % high * fold_rows[a], fold_rows[a]),
+            pl.ds(j // high * fold_width[a], fold_width[a]),
+        )
         partial, arrived, across, total = (
-            ref.at[j] if k < 3 else ref.at[:, pl.ds(j * fold_width[a], fold_width[a])]
+            ref.at[j] if k < 3 else ref.at[place]
             for k, ref in enumerate(fold_refs[a])
         )
         return partial, arrived, across, total
@@ -209,19 +215,13 @@
     r.misc_weight[0:NS, :] = r.state_weight[...]
     r.misc_weight[NS : NS + H, :] = r.step_weight[...]
     normed_all = r.normed[...]
-    for j in range(HI // 256):
-        cols = slice(256 * j, 256 * j + 256)
-        value = dg(normed_all, r.inner_weight[:, cols], 1, 0)
-        r.inner_ext[2 * j, PAD : PAD + T, :] = value[:, :LANES]
-        r.inner_ext[2 * j + 1, PAD : PAD + T, :] = value[:, LANES:]
     r.misc_ext[0, PAD : PAD + T, :] = dg(normed_all, r.misc_weight[...], 1, 1)
-
     stage("barrier")
     pl.semaphore_wait(barrier, n_seq - 1 + n_tp - 1)
-    stage("gate_projection")
+    stage("inner_projection")
     right = ((seq + 1) % n_seq, tp)
     left = ((seq + n_seq - 1) % n_seq, tp)
-    rim = [
+    misc_rim, inner_rim = [
         remote(
             ref.at[:, pl.ds(T, PAD)],
             ref.at[:, pl.ds(0, PAD)],
@@ -229,11 +229,17 @@
             r.rim_recv.at[k],
             right,
         )
-        for k, ref in enumerate((r.inner_ext, r.misc_ext))
+        for k, ref in enumerate((r.misc_ext, r.inner_ext))
     ]
-    for copy in rim:
-        copy.start()
-    waits.extend(rim)
+    waits.extend((misc_rim, inner_rim))
+    misc_rim.start()
+    for j in range(HI // 256):
+        cols = slice(256 * j, 256 * j + 256)
+        value = dg(normed_all, r.inner_weight[:, cols], 1, 0)
+        r.inner_ext[2 * j, PAD : PAD + T, :] = value[:, :LANES]
+        r.inner_ext[2 * j + 1, PAD : PAD + T, :] = value[:, LANES:]
+    inner_rim.start()
+    stage("gate_projection")
     for j in range(HI // 256):
         cols = slice(256 * j, 256 * j + 256)
         r.gate_pre[:, cols] = dg(normed_all, r.gate_weight[:, cols], 1, 0)
@@ -257,8 +263,7 @@
     r.misc_taps[CONV : CONV + 1, 0:NS] = r.state_conv_bias[...].reshape(1, NS)
     r.inner_bias[...] = r.inner_conv_bias[...].reshape(1, HI)
     stage("rim_wait")
-    for copy in rim:
-        copy.wait_recv()
+    misc_rim.wait_recv()
     stage("conv")
 
     def misc_conv_rows(i, _):
@@ -299,6 +304,7 @@
             r.act[rows, lanes] = (value * jax.nn.sigmoid(value)).astype(bf)
         return 0
 
+    inner_rim.wait_recv()
     lax.fori_loop(0, T // ROWS, inner_conv_rows, 0)
 
     stage("decays")
@@ -441,7 +447,8 @@
         result = None
         for s in range(2):
             h = 2 * p + s
-            weight, rest = halves(r.decays[c, h] * r.scores[c] * r.step_rows[pl.ds(h, 1), rows])
+            stepped = r.decays[c, h] * r.step_rows[pl.ds(h, 1), rows]
+            weight, rest = halves(stepped * r.scores[c])
             part = jnp.where(low, x, zero) if s == 0 else jnp.where(low, zero, x)
             term = dg(weight, part, 1, 0) + dg(rest, part, 1, 0)
             result = term if s == 0 else result + term
@@ -471,6 +478,15 @@
     enter_wait = spread(
         "seq", lambda d: r.enter_send.at[d], lambda d: block(r.enter_state, d), r.enter_ss, r.enter_rs
     )
+    stage("turned_weights")
+
+    def turned_weight(i, _):
+        c = i // H
+        h = i % H
+        r.turned[c, h] = (r.decays[c, h] * r.scores[c]).T.astype(bf)
+        return 0
+
+    lax.fori_loop(0, NC * H, turned_weight, 0)
     stage("enter_wait")
     enter_wait()
     stage("readout")
@@ -497,7 +513,6 @@
         heads = r.mixed[rows, :] + skip_row * r.act[rows, :].astype(f32)
         gate = r.gate_pre[rows, :]
         gated = heads * (gate * jax.nn.sigmoid(gate))
-        r.heads_out[rows, :] = heads
         r.gated[rows, :] = gated
         scaled = r.norm_grad[rows, :] * r.gain_row[...]
         squares = gated * gated
@@ -562,7 +577,7 @@
         r.sum_acc[0] = r.sum_acc[0] + fold8(grad * unit)
         gated_grad = norm * (grad * gain) - gated * back
         heads_grad = gated_grad * (gate * sigma)
-        heads = r.heads_out[rows, :]
+        heads = r.mixed[rows, :] + skip_row * r.act[rows, :].astype(f32)
         r.gate_grad[rows, :] = (
             gated_grad * heads * (sigma * (1.0 + gate * (1.0 - sigma)))
         ).astype(bf)
@@ -590,10 +605,12 @@
         "seq", lambda d: block(r.grad_send, d), lambda d: r.grad_recv.at[d], r.grad_ss, r.grad_rs
     )
     stage("out_projection")
-    for j in range(fold_pieces[0]):
-        cols = slice(fold_width[0] * j, fold_width[0] * (j + 1))
-        r.branch[j] = dg(r.gated_norm[...], r.out_weight[:, cols], 1, 0).astype(bf)
-        fold_start(0, j)
+    for j in range(D // 256):
+        value = dg(r.gated_norm[...], r.out_weight[:, 256 * j : 256 * j + 256], 1, 0).astype(bf)
+        for k in range(256 // fold_width[0]):
+            at = j * (256 // fold_width[0]) + k
+            r.branch[at] = value[:, k * fold_width[0] : (k + 1) * fold_width[0]]
+            fold_start(0, at)
     stage("inside_back")
     r.score_grad[...] = jnp.zeros_like(r.score_grad)
 
@@ -606,24 +623,33 @@
         dy = r.dy[rows, lanes]
         dy_rest = r.dy_rest[rows, lanes]
         zero = jnp.zeros_like(dy)
+        x_turned, dy_turned = pltpu.roll(x, P_, 1), pltpu.roll(dy_rest, P_, 1)
         result = None
         for s in range(2):
             h = 2 * p + s
-            decay = r.decays[c, h]
-            weight, rest = halves(decay * r.scores[c])
-
-            def masked(v):
-                return jnp.where(low, v, zero) if s == 0 else jnp.where(low, zero, v)
-
-            part, part_rest = masked(dy), masked(dy_rest)
-            pairs = dg(part, x, 1, 1) + dg(part_rest, x, 1, 1)
-            r.score_grad[c] = r.score_grad[c] + pairs * (decay * r.step_rows[pl.ds(h, 1), rows])
-            term = dg(weight, part, 0, 0) + dg(rest, part, 0, 0) + dg(weight, part_rest, 0, 0)
+            ours = low if s == 0 else jnp.logical_not(low)
+            pairs = dg(jnp.where(ours, dy, dy_turned), jnp.where(ours, x, x_turned), 1, 1)
+            r.score_grad[c] = r.score_grad[c] + pairs * (r.decays[c, h] * r.step_rows[pl.ds(h, 1), rows])
+            term = dg(r.turned[c, h], jnp.where(ours, dy, zero), 1, 0)
             result = term if s == 0 else result + term
         r.x_inside[rows, lanes] = result
         return 0
 
     lax.fori_loop(0, NC * NP, inside_back, 0)
+
+    stage("poll_at_grad_wait")
+    fold_in(0, 0)
+    stage("grad_wait")
+    grad_wait()
+    stage("leave_scan")
+    running = jnp.zeros((R, N), f32)
+    for d in reversed(range(n_seq)):
+        r.leave_send[d] = running
+        running = decay_of(d) * running + r.grad_recv[d]
+    r.leave_grad[own_rows, :] = r.leave_send[seq]
+    leave_wait = spread(
+        "seq", lambda d: r.leave_send.at[d], lambda d: block(r.leave_grad, d), r.leave_ss, r.leave_rs
+    )
 
     stage("query_grad")
     for c in range(NC):
@@ -656,18 +682,8 @@
             pl.when((tp + d) % n_tp // shards == group)(shared_copy(d).start)
 
     pack_shared(r.query_grad, 1)
-    stage("grad_wait")
-    grad_wait()
-    stage("leave_scan")
-    running = jnp.zeros((R, N), f32)
-    for d in reversed(range(n_seq)):
-        r.leave_send[d] = running
-        running = decay_of(d) * running + r.grad_recv[d]
-    r.leave_grad[own_rows, :] = r.leave_send[seq]
-    leave_wait = spread(
-        "seq", lambda d: r.leave_send.at[d], lambda d: block(r.leave_grad, d), r.leave_ss, r.leave_rs
-    )
-
+    stage("poll_at_weights_one")
+    fold_in(0, 1)
     stage("weights_one")
     def weight_rows(i, _):
         cols = pl.ds(pl.multiple_of(i * LANES, LANES), LANES)
@@ -732,9 +748,9 @@
         return value
 
     pair_start(0)
-    stage("poll_one")
-    fold_in(0, 0)
-    fold_in(0, 1)
+    stage("poll_at_leave_wait")
+    fold_in(0, 2)
+    fold_middle(0, 0)
     stage("leave_wait")
     leave_wait()
     stage("leave")
@@ -763,8 +779,14 @@
         )
 
     pack_shared(r.key_grad, 0)
+    stage("poll_at_chip_one")
+    fold_in(0, 3)
+    fold_middle(0, 1)
     stage("chip_one")
     chip_start(0)
+    stage("poll_at_x_grads")
+    fold_in(0, 4)
+    fold_middle(0, 2)
     stage("x_grads")
     r.head_sum_two[...] = (
         iota((HI, LANES), 0) // P_ + H == iota((HI, LANES), 1)
@@ -823,6 +845,9 @@
         [jnp.zeros((NS, T), f32), step_pre_grad, jnp.zeros((LANES - NS - H, T), f32)], axis=0
     ).T
 
+    stage("poll_at_conv_back")
+    fold_in(0, 5)
+    fold_middle(0, 3)
     stage("conv_back")
     def after_masks(base):
         position = first_token + base + iota((ROWS, LANES), 0)
@@ -866,17 +891,16 @@
         return 0
 
     lax.fori_loop(0, T // ROWS - 1, inner_back_rows, 0)
-    stage("poll_two")
-    fold_in(0, 2)
-    fold_middle(0, 0)
+    stage("poll_at_halo_one_wait")
+    fold_in(0, 6)
+    fold_middle(0, 4)
     stage("halo_one_wait")
     halo_one.wait_recv()
     stage("inner_back_last")
     inner_back_rows(T // ROWS - 1, 0)
 
-    stage("poll_three")
-    fold_in(0, 3)
-    fold_middle(0, 1)
+    stage("poll_at_shared_wait")
+    fold_middle(0, 5)
     stage("shared_wait")
     for d in range(1, n_tp):
         shared_copy(d, True).wait_recv()
@@ -895,6 +919,8 @@
     )
     halo_two.start()
     waits.append(halo_two)
+    stage("poll_at_misc_back")
+    fold_in(0, 7)
     stage("misc_back")
     r.misc_acc[...] = jnp.zeros_like(r.misc_acc)
     r.step_cols[...] = step_cols
@@ -920,8 +946,10 @@
     stage("misc_back_last")
     misc_back_rows(T // ROWS - 1, 0)
 
+    stage("poll_at_normed_grad")
+    fold_middle(0, 6)
     stage("normed_grad")
-    width = fold_width[1]
+    width, tall = fold_width[1], fold_rows[1]
     for j in range(D // 256):
         cols = slice(256 * j, 256 * (j + 1))
         value = (
@@ -929,13 +957,17 @@
             + dg(r.inner_grad[...], r.inner_weight[cols, :], 1, 1)
             + dg(r.misc_grad[...], r.misc_weight[:, cols], 1, 0)
         )
+        value_low = value.astype(bf)
         for k in range(256 // width):
-            at = j * (256 // width) + k
-            r.normed_part[at] = value[:, k * width : k * width + width].astype(bf)
-            fold_start(1, at)
+            for m in range(T // tall):
+                at = (j * (256 // width) + k) * (T // tall) + m
+                r.normed_part[at] = value_low[m * tall : m * tall + tall, k * width : k * width + width]
+                fold_start(1, at)
         hats = r.block_input[:, cols].astype(f32) * jnp.concatenate([r.inverse[...]] * 2, axis=1)
         r.gain_part[:, cols] = fold8(value * hats)
 
+    stage("poll_at_small_sums")
+    fold_middle(0, 7)
     stage("small_sums")
 
     def row_of(v):
@@ -963,9 +995,6 @@
     small_wait = spread(
         "seq", lambda d: r.small_send, lambda d: r.small_recv.at[d], r.small_ss, r.small_rs
     )
-    stage("poll_four")
-    fold_middle(0, 2)
-    fold_middle(0, 3)
     stage("weights_two")
 
     def weight_rows_two(i, _):
@@ -974,18 +1003,20 @@
         r.wg_two[cols, HI : HI + LANES] = dg(r.normed[:, cols], r.misc_grad[...], 0, 0).astype(bf)
         return 0
 
-    lax.fori_loop(0, D // LANES, weight_rows_two, 0)
+    lax.fori_loop(0, D // LANES // 2, weight_rows_two, 0)
+    fold_in(1, 0)
+    lax.fori_loop(D // LANES // 2, D // LANES, weight_rows_two, 0)
     pair_start(1)
     stage("folds")
     last = fold_pieces[1]
-    for j in range(last + 1):
-        if j < last:
+    for j in range(last + 2):
+        if 0 < j < last:
             fold_in(1, j)
-        if j > 0:
-            fold_middle(1, j - 1)
-        if j == 0:
+        if j > 1:
+            fold_middle(1, j - 2)
+        if j == 2:
             chip_start(1)
-        if j == 1:
+        if j == 4:
             small_wait()
             total = r.small_recv[0]
             for d in range(1, n_seq):
@@ -999,18 +1030,17 @@
                 r.gain_ss,
                 r.gain_rs,
             )
-        if j == last - 1:
-            stage("weight_sums")
-            r.sum_one[...] = chip_sum(0)
-            r.sum_two[...] = chip_sum(1)
-            gain_wait()
-            gains = r.gain_recv[0]
-            for t in range(1, n_tp):
-                gains = gains + r.gain_recv[t]
-            r.gain_total[...] = gains
-            stage("folds_last")
     for j in range(fold_pieces[0]):
         fold_end(0, j)
+    stage("weight_sums")
+    r.sum_one[...] = chip_sum(0)
+    r.sum_two[...] = chip_sum(1)
+    gain_wait()
+    gains = r.gain_recv[0]
+    for t in range(1, n_tp):
+        gains = gains + r.gain_recv[t]
+    r.gain_total[...] = gains
+    stage("folds_last")
     for j in range(fold_pieces[1]):
         fold_end(1, j)
     stage("drain")
@@ -1194,9 +1224,9 @@
         scores=((NC, Q, Q), f32),
         score_grad=((NC, Q, Q), f32),
         decays=((NC, H, Q, Q), f32),
+        turned=((NC, H, Q, Q), bf),
         mixed=((T, HI), f32),
         norm_grad=((T, HI), f32),
-        heads_out=((T, HI), f32),
         gated=((T, HI), f32),
         squares=((T, LANES), f32),
         products=((T, LANES), f32),
@@ -1242,12 +1272,12 @@
         step_cols=((T, LANES), f32),
         misc_grad=((T, LANES), bf),
         misc_acc=((CONV + 1, 8, LANES), f32),
-        normed_part=((8, T, D // 8), bf),
-        normed_in=((8, T, D // 8), bf),
-        normed_across=((8, T, D // 8), bf),
-        branch=((4, T, D // 4), bf),
-        branch_in=((4, T, D // 4), bf),
-        branch_across=((4, T, D // 4), bf),
+        normed_part=((16, T // 2, D // 8), bf),
+        normed_in=((16, T // 2, D // 8), bf),
+        normed_across=((16, T // 2, D // 8), bf),
+        branch=((8, T, D // 8), bf),
+        branch_in=((8, T, D // 8), bf),
+        branch_across=((8, T, D // 8), bf),
         gain_part=((8, D), f32),
         small_send=((16, HI), f32),
         small_recv=((n_seq, 16, HI), f32),
@@ -1262,8 +1292,8 @@
         pair_rs=(2, n_seq // 2),
         chip_ss=(2, n_seq // 2 - 1),
         chip_rs=(2, n_seq // 2 - 1),
-        fold_ss=(3, 12),
-        fold_rs=(3, 12),
+        fold_ss=(3, 24),
+        fold_rs=(3, 24),
     )
     for name in ("state", "sums", "shared", "gain"):
         semaphores[name + "_ss"] = (n_tp - 1,)
@@ -1282,7 +1312,7 @@
         scratch_shapes=[pltpu.VMEM(s, t) for s, t in scratch.values()]
         + [pltpu.SemaphoreType.DMA(s) for s in semaphores.values()],
         compiler_params=pltpu.CompilerParams(
-            collective_id=0, has_side_effects=True, vmem_limit_bytes=60 * 2**20
+            collective_id=0, has_side_effects=True, vmem_limit_bytes=61 * 2**20
         ),
     )(*given.values())
     tall = ("block_input", "out_cotangent", "branch_sum", "normed_sum", "block_output", "input_grad")

time: 118 us -> 115 us (0.975)
  Pallas kernels: 117 us -> 114 us
    pallas_call x1, Pallas kernels: 111 us -> 107 us  [local(): pl.pallas_call(functools.partial(kernel, (n_seq, n_tp, T, D, HI, H, NS),...]
where the time goes in v3:
time: 115 us; the launch traced here: 114 us
  Pallas kernels  114 us (99%)
    pallas_call x1, Pallas kernels, local(): pl.pallas_call(functools.partial(kernel, (n_seq, n_tp, T, D, HI, H, NS),...  107 us
    pallas_call x1, Pallas kernels, local(): pl.pallas_call(functools.partial(finish, (T, D, HI, H, NS), needed + SUMS...  6.1 us

profile of v3, /device:TPU:0, one launch (start us, length us, event | category | flops | bytes accessed | tf_op | source)
XLA Modules:
  0.0 114.4 jit_solution(6499422710175734887)
XLA Ops:
  0.7 107.5 %shard_map.288 = (bf16[512,1024]{1,0:T(8,128)(2,1)}, bf16[512,1024]{1,0:T(8,128)(2,1)}, f32[128,1024]{1,0:T(8,128)}, f32[128,640]{1,0:T(8,128)}, f32[16,512]{1,0:T(8,128)}, /*index=5*/f32[8,512]{1,0:T(8,128)}) custom-call(bf16[512,1024]{1,0:T(8,128)(2,1)} %refs_0_.3, s32[4]{0:T(128)} %refs_1_.2, f32[1024]{0:T(1024)} %refs_1_.3, bf16[1024,512]{1,0:T(8,128)(2,1)} %refs_3_.1, ...), custom_call_target="tpu_custom_call" | custom-call | tf_op jit(solution)/shard_map/pallas_call | solution.py:1307
  108.2 6.1 %shard_map.289 = (bf16[512,1024]{1,0:T(8,128)(2,1)}, f32[512,1024]{1,0:T(8,128)}, f32[1024]{0:T(1024)}, f32[128,512]{1,0:T(8,128)}, f32[128,512]{1,0:T(8,128)}, ...) custom-call(bf16[512,1024]{1,0:T(8,128)(2,1)} %refs_0_.3, ...), custom_call_target="tpu_custom_call" | custom-call | tf_op jit(solution)/shard_map/pallas_call | solution.py:1326

commit v4 on v3

--- a/solution.py
+++ b/solution.py
@@ -58,6 +58,9 @@
 
 def iota(shape, dim):
     return lax.broadcasted_iota(i32, shape, dim)
+
+
+LOADED = ("inner_weight", "gate_weight", "out_weight", "out_cotangent")
 
 
 def kernel(sizes, names, *refs):
@@ -85,6 +88,10 @@
         )
 
     waits = []
+    loads = {}
+    for k, n in enumerate(LOADED):
+        loads[n] = pltpu.make_async_copy(getattr(r, n + "_hbm"), getattr(r, n), r.load_sems.at[k])
+        loads[n].start()
     half = n_tp // 2
     inner = jnp.where(tp < half, tp + 1, tp - 1)
     outer = jnp.where(tp < half, tp - 1, tp + 1)
@@ -235,6 +242,8 @@
     misc_rim.start()
     for j in range(HI // 256):
         cols = slice(256 * j, 256 * j + 256)
+        if j == 0:
+            loads["inner_weight"].wait()
         value = dg(normed_all, r.inner_weight[:, cols], 1, 0)
         r.inner_ext[2 * j, PAD : PAD + T, :] = value[:, :LANES]
         r.inner_ext[2 * j + 1, PAD : PAD + T, :] = value[:, LANES:]
@@ -242,6 +251,8 @@
     stage("gate_projection")
     for j in range(HI // 256):
         cols = slice(256 * j, 256 * j + 256)
+        if j == 0:
+            loads["gate_weight"].wait()
         r.gate_pre[:, cols] = dg(normed_all, r.gate_weight[:, cols], 1, 0)
 
     stage("convolutions")
@@ -458,6 +469,9 @@
     lax.fori_loop(0, NC * NP, inside, 0)
     for j in range(HI // 256):
         cols = slice(256 * j, 256 * j + 256)
+        if j == 0:
+            loads["out_weight"].wait()
+            loads["out_cotangent"].wait()
         r.norm_grad[:, cols] = dg(r.out_cotangent[...], r.out_weight[cols, :], 1, 1)
 
     stage("entering")
@@ -563,6 +577,22 @@
         high, lowv = halves(v)
         return dg(high, which, 1, 0) + dg(lowv, which, 1, 0)
 
+    def gated_norm_rows(i, _):
+        rows = pl.ds(pl.multiple_of(i * ROWS, ROWS), ROWS)
+        unit = r.gated[rows, :] * tile4(r.norm_col[rows, :])
+        r.gated_norm[rows, :] = (unit * r.gain_row[...]).astype(bf)
+        return 0
+
+    lax.fori_loop(0, T // ROWS, gated_norm_rows, 0)
+    stage("out_projection")
+    for j in range(D // 256):
+        value = dg(r.gated_norm[...], r.out_weight[:, 256 * j : 256 * j + 256], 1, 0).astype(bf)
+        for k in range(256 // fold_width[0]):
+            at = j * (256 // fold_width[0]) + k
+            r.branch[at] = value[:, k * fold_width[0] : (k + 1) * fold_width[0]]
+            fold_start(0, at)
+    stage("back_rows")
+
     def back_rows(i, _):
         rows = pl.ds(pl.multiple_of(i * ROWS, ROWS), ROWS)
         norm = tile4(r.norm_col[rows, :])
@@ -573,7 +603,6 @@
         gate = r.gate_pre[rows, :]
         sigma = jax.nn.sigmoid(gate)
         unit = gated * norm
-        r.gated_norm[rows, :] = (unit * gain).astype(bf)
         r.sum_acc[0] = r.sum_acc[0] + fold8(grad * unit)
         gated_grad = norm * (grad * gain) - gated * back
         heads_grad = gated_grad * (gate * sigma)
@@ -604,13 +633,6 @@
     grad_wait = spread(
         "seq", lambda d: block(r.grad_send, d), lambda d: r.grad_recv.at[d], r.grad_ss, r.grad_rs
     )
-    stage("out_projection")
-    for j in range(D // 256):
-        value = dg(r.gated_norm[...], r.out_weight[:, 256 * j : 256 * j + 256], 1, 0).astype(bf)
-        for k in range(256 // fold_width[0]):
-            at = j * (256 // fold_width[0]) + k
-            r.branch[at] = value[:, k * fold_width[0] : (k + 1) * fold_width[0]]
-            fold_start(0, at)
     stage("inside_back")
     r.score_grad[...] = jnp.zeros_like(r.score_grad)
 
@@ -782,8 +804,7 @@
     stage("poll_at_chip_one")
     fold_in(0, 3)
     fold_middle(0, 1)
-    stage("chip_one")
-    chip_start(0)
+    stage("after_keys")
     stage("poll_at_x_grads")
     fold_in(0, 4)
     fold_middle(0, 2)
@@ -919,6 +940,8 @@
     )
     halo_two.start()
     waits.append(halo_two)
+    stage("chip_one")
+    chip_start(0)
     stage("poll_at_misc_back")
     fold_in(0, 7)
     stage("misc_back")
@@ -1016,7 +1039,7 @@
             fold_middle(1, j - 2)
         if j == 2:
             chip_start(1)
-        if j == 4:
+        if j == 10:
             small_wait()
             total = r.small_recv[0]
             for d in range(1, n_seq):
@@ -1301,13 +1324,18 @@
     for name in ("decay", "end", "enter", "grad", "leave", "small"):
         semaphores[name + "_ss"] = (n_seq - 1,)
         semaphores[name + "_rs"] = (n_seq - 1,)
-    names = INPUTS + SUMS + tuple(scratch) + tuple(semaphores)
+    scratch.update({n: (given[n].shape, bf) for n in LOADED})
+    semaphores["load_sems"] = (len(LOADED),)
+    names = tuple(n + "_hbm" if n in LOADED else n for n in INPUTS) + SUMS + tuple(scratch) + tuple(semaphores)
     vmem = pl.BlockSpec(memory_space=pltpu.VMEM)
     smem = pl.BlockSpec(memory_space=pltpu.SMEM)
     totals = pl.pallas_call(
         functools.partial(kernel, (n_seq, n_tp, T, D, HI, H, NS), names),
         out_shape=tuple(jax.ShapeDtypeStruct(s, t) for s, t in sums),
-        in_specs=[smem if n == "scene_lengths" else vmem for n in INPUTS],
+        in_specs=[
+            smem if n == "scene_lengths" else pl.BlockSpec(memory_space=pl.ANY) if n in LOADED else vmem
+            for n in INPUTS
+        ],
         out_specs=tuple(vmem for _ in sums),
         scratch_shapes=[pltpu.VMEM(s, t) for s, t in scratch.values()]
         + [pltpu.SemaphoreType.DMA(s) for s in semaphores.values()],
@@ -1316,7 +1344,7 @@
         ),
     )(*given.values())
     tall = ("block_input", "out_cotangent", "branch_sum", "normed_sum", "block_output", "input_grad")
-    steps = 4
+    steps = 2
     by_rows = pl.BlockSpec((T // steps, D), lambda i: (i, 0))
 
     def whole(shape):

time: 115 us -> 111 us (0.965)
  Pallas kernels: 114 us -> 110 us
    pallas_call x1, Pallas kernels: 107 us -> 104 us  [local(): pl.pallas_call(functools.partial(kernel, (n_seq, n_tp, T, D, HI, H, NS),...]
where the time goes in v4:
time: 111 us
  Pallas kernels  110 us (99%)
    pallas_call x1, Pallas kernels, local(): pl.pallas_call(functools.partial(kernel, (n_seq, n_tp, T, D, HI, H, NS),...  104 us
    pallas_call x1, Pallas kernels, local(): pl.pallas_call(functools.partial(finish, (T, D, HI, H, NS), needed + SUMS...  5.63 us

profile of v4, /device:TPU:0, one launch (start us, length us, event | category | flops | bytes accessed | tf_op | source)
XLA Modules:
  0.0 110.9 jit_solution(9900710334152704651)
XLA Ops:
  0.7 104.4 %shard_map.288 = (bf16[512,1024]{1,0:T(8,128)(2,1)}, bf16[512,1024]{1,0:T(8,128)(2,1)}, f32[128,1024]{1,0:T(8,128)}, f32[128,640]{1,0:T(8,128)}, f32[16,512]{1,0:T(8,128)}, /*index=5*/f32[8,512]{1,0:T(8,128)}) custom-call(bf16[512,1024]{1,0:T(8,128)(2,1)} %refs_0_.3, s32[4]{0:T(128)} %refs_1_.2, f32[1024]{0:T(1024)} %refs_1_.3, bf16[1024,512]{1,0:T(8,128)(2,1)} %refs_3_.1, ...), custom_call_target="tpu_custom_call" | custom-call | tf_op jit(solution)/shard_map/pallas_call | solution.py:1332
  105.1 5.6 %shard_map.289 = (bf16[512,1024]{1,0:T(8,128)(2,1)}, f32[512,1024]{1,0:T(8,128)}, f32[1024]{0:T(1024)}, f32[128,512]{1,0:T(8,128)}, f32[128,512]{1,0:T(8,128)}, ...) custom-call(bf16[512,1024]{1,0:T(8,128)(2,1)} %refs_0_.3, ...), custom_call_target="tpu_custom_call" | custom-call | tf_op jit(solution)/shard_map/pallas_call | solution.py:1354

commit v5 on v4

--- a/solution.py
+++ b/solution.py
@@ -657,10 +657,13 @@
         r.x_inside[rows, lanes] = result
         return 0
 
-    lax.fori_loop(0, NC * NP, inside_back, 0)
+    lax.fori_loop(0, 4, inside_back, 0)
+    fold_in(0, 0)
+    lax.fori_loop(4, 7, inside_back, 0)
+    fold_in(0, 1)
+    lax.fori_loop(7, NC * NP, inside_back, 0)
 
     stage("poll_at_grad_wait")
-    fold_in(0, 0)
     stage("grad_wait")
     grad_wait()
     stage("leave_scan")
@@ -676,9 +679,10 @@
     stage("query_grad")
     for c in range(NC):
         rows = slice(c * Q, c * Q + Q)
-        score_low = r.score_grad[c].astype(bf)
+        score_low, score_rest = halves(r.score_grad[c])
         r.query_grad[rows, :] = (
             dg(score_low, r.keys[rows, :], 1, 0)
+            + dg(score_rest, r.keys[rows, :], 1, 0)
             + dg(r.dy_enter[rows, :], r.state_in_low[c], 1, 0)
             + dg(r.dy_enter_rest[rows, :], r.state_in_low[c], 1, 0)
             + dg(r.dy_enter[rows, :], r.state_in_rest[c], 1, 0)
@@ -705,7 +709,7 @@
 
     pack_shared(r.query_grad, 1)
     stage("poll_at_weights_one")
-    fold_in(0, 1)
+    fold_in(0, 2)
     stage("weights_one")
     def weight_rows(i, _):
         cols = pl.ds(pl.multiple_of(i * LANES, LANES), LANES)
@@ -771,8 +775,8 @@
 
     pair_start(0)
     stage("poll_at_leave_wait")
-    fold_in(0, 2)
     fold_middle(0, 0)
+    fold_in(0, 3)
     stage("leave_wait")
     leave_wait()
     stage("leave")
@@ -792,9 +796,10 @@
         high, lowv = halves(grad * r.state_in[c])
         pair = dg(expand[0:H], high, 1, 0) + dg(expand[0:H], lowv, 1, 0)
         carry_terms[c] = chunk_decay[c] * jnp.sum(pair, axis=1, keepdims=True)
-        score_low = r.score_grad[c].astype(bf)
+        score_low, score_rest = halves(r.score_grad[c])
         r.key_grad[rows, :] = (
             dg(score_low, queries, 0, 0)
+            + dg(score_rest, queries, 0, 0)
             + dg(r.xt[rows, :], grad_low, 1, 0)
             + dg(r.xt_rest[rows, :], grad_low, 1, 0)
             + dg(r.xt[rows, :], grad_rest, 1, 0)
@@ -802,7 +807,6 @@
 
     pack_shared(r.key_grad, 0)
     stage("poll_at_chip_one")
-    fold_in(0, 3)
     fold_middle(0, 1)
     stage("after_keys")
     stage("poll_at_x_grads")
@@ -922,6 +926,7 @@
 
     stage("poll_at_shared_wait")
     fold_middle(0, 5)
+    fold_in(0, 7)
     stage("shared_wait")
     for d in range(1, n_tp):
         shared_copy(d, True).wait_recv()
@@ -943,7 +948,7 @@
     stage("chip_one")
     chip_start(0)
     stage("poll_at_misc_back")
-    fold_in(0, 7)
+    fold_middle(0, 6)
     stage("misc_back")
     r.misc_acc[...] = jnp.zeros_like(r.misc_acc)
     r.step_cols[...] = step_cols
@@ -970,7 +975,6 @@
     misc_back_rows(T // ROWS - 1, 0)
 
     stage("poll_at_normed_grad")
-    fold_middle(0, 6)
     stage("normed_grad")
     width, tall = fold_width[1], fold_rows[1]
     for j in range(D // 256):

time: 111 us -> 111 us (level)
  no operation moved by 1% of the time
where the time goes in v5:
time: 111 us
  Pallas kernels  110 us (99%)
    pallas_call x1, Pallas kernels, local(): pl.pallas_call(functools.partial(kernel, (n_seq, n_tp, T, D, HI, H, NS),...  104 us
    pallas_call x1, Pallas kernels, local(): pl.pallas_call(functools.partial(finish, (T, D, HI, H, NS), needed + SUMS...  5.63 us

profile of v5, /device:TPU:0, one launch (start us, length us, event | category | flops | bytes accessed | tf_op | source)
XLA Modules:
  0.0 110.5 jit_solution(5046673464949702951)
XLA Ops:
  0.7 104.1 %shard_map.288 = (bf16[512,1024]{1,0:T(8,128)(2,1)}, bf16[512,1024]{1,0:T(8,128)(2,1)}, f32[128,1024]{1,0:T(8,128)}, f32[128,640]{1,0:T(8,128)}, f32[16,512]{1,0:T(8,128)}, /*index=5*/f32[8,512]{1,0:T(8,128)}) custom-call(bf16[512,1024]{1,0:T(8,128)(2,1)} %refs_0_.3, s32[4]{0:T(128)} %refs_1_.2, f32[1024]{0:T(1024)} %refs_1_.3, bf16[1024,512]{1,0:T(8,128)(2,1)} %refs_3_.1, ...), custom_call_target="tpu_custom_call" | custom-call | tf_op jit(solution)/shard_map/pallas_call | solution.py:1336
  104.7 5.6 %shard_map.289 = (bf16[512,1024]{1,0:T(8,128)(2,1)}, f32[512,1024]{1,0:T(8,128)}, f32[1024]{0:T(1024)}, f32[128,512]{1,0:T(8,128)}, f32[128,512]{1,0:T(8,128)}, ...) custom-call(bf16[512,1024]{1,0:T(8,128)(2,1)} %refs_0_.3, ...), custom_call_target="tpu_custom_call" | custom-call | tf_op jit(solution)/shard_map/pallas_call | solution.py:1358

commit v6 on v5

--- a/solution.py
+++ b/solution.py
@@ -545,11 +545,16 @@
     lax.fori_loop(0, T // ROWS, gated_rows, 0)
     square_row = jnp.sum(r.squares[...].T, axis=0, keepdims=True)
     product_row = jnp.sum(r.products[...].T, axis=0, keepdims=True)
-    r.sums_send[...] = jnp.where(
-        iota((8, T), 0) == 0,
-        jnp.broadcast_to(square_row, (8, T)),
-        jnp.broadcast_to(product_row, (8, T)),
-    )
+    spans = T // LANES
+    tile_row = iota((2 * spans, LANES), 0)
+    packed_sums = jnp.zeros((2 * spans, LANES), f32)
+    for k in range(spans):
+        lanes = slice(k * LANES, k * LANES + LANES)
+        for at, row in ((k, square_row), (spans + k, product_row)):
+            packed_sums = jnp.where(
+                tile_row == at, jnp.broadcast_to(row[:, lanes], (2 * spans, LANES)), packed_sums
+            )
+    r.sums_send[...] = packed_sums
     r.sums_recv[tp] = r.sums_send[...]
     sums_wait = spread(
         "tp", lambda t: r.sums_send, lambda t: r.sums_recv.at[t], r.sums_ss, r.sums_rs
@@ -561,8 +566,10 @@
     for t in range(1, n_tp):
         sums = sums + r.sums_recv[t]
     count = HI * n_tp
-    norm_row = lax.rsqrt(sums[0:1] / count + epsilon)
-    back_row = norm_row * norm_row * norm_row * (sums[1:2] / count)
+    squares = jnp.concatenate([sums[k : k + 1] for k in range(spans)], axis=1)
+    products = jnp.concatenate([sums[spans + k : spans + k + 1] for k in range(spans)], axis=1)
+    norm_row = lax.rsqrt(squares / count + epsilon)
+    back_row = norm_row * norm_row * norm_row * (products / count)
     r.norm_col[...] = jnp.broadcast_to(norm_row, (LANES, T)).T
     r.back_col[...] = jnp.broadcast_to(back_row, (LANES, T)).T
 
@@ -1257,8 +1264,8 @@
         gated=((T, HI), f32),
         squares=((T, LANES), f32),
         products=((T, LANES), f32),
-        sums_send=((8, T), f32),
-        sums_recv=((n_tp, 8, T), f32),
+        sums_send=((2 * T // LANES, LANES), f32),
+        sums_recv=((n_tp, 2 * T // LANES, LANES), f32),
         norm_col=((T, LANES), f32),
         back_col=((T, LANES), f32),
         head_sum=((HI, LANES), bf),

time: 111 us -> 110 us (level)
  no operation moved by 1% of the time
where the time goes in v6:
time: 110 us
  Pallas kernels  109 us (99%)
    pallas_call x1, Pallas kernels, local(): pl.pallas_call(functools.partial(kernel, (n_seq, n_tp, T, D, HI, H, NS),...  104 us
    pallas_call x1, Pallas kernels, local(): pl.pallas_call(functools.partial(finish, (T, D, HI, H, NS), needed + SUMS...  5.63 us

profile of v6, /device:TPU:0, one launch (start us, length us, event | category | flops | bytes accessed | tf_op | source)
XLA Modules:
  0.0 110.3 jit_solution(1113340683327617563)
XLA Ops:
  0.7 103.9 %shard_map.288 = (bf16[512,1024]{1,0:T(8,128)(2,1)}, bf16[512,1024]{1,0:T(8,128)(2,1)}, f32[128,1024]{1,0:T(8,128)}, f32[128,640]{1,0:T(8,128)}, f32[16,512]{1,0:T(8,128)}, /*index=5*/f32[8,512]{1,0:T(8,128)}) custom-call(bf16[512,1024]{1,0:T(8,128)(2,1)} %refs_0_.3, s32[4]{0:T(128)} %refs_1_.2, f32[1024]{0:T(1024)} %refs_1_.3, bf16[1024,512]{1,0:T(8,128)(2,1)} %refs_3_.1, ...), custom_call_target="tpu_custom_call" | custom-call | tf_op jit(solution)/shard_map/pallas_call | solution.py:1343
  104.5 5.6 %shard_map.289 = (bf16[512,1024]{1,0:T(8,128)(2,1)}, f32[512,1024]{1,0:T(8,128)}, f32[1024]{0:T(1024)}, f32[128,512]{1,0:T(8,128)}, f32[128,512]{1,0:T(8,128)}, ...) custom-call(bf16[512,1024]{1,0:T(8,128)(2,1)} %refs_0_.3, ...), custom_call_target="tpu_custom_call" | custom-call | tf_op jit(solution)/shard_map/pallas_call | solution.py:1365
